TPU v7x, 512 devices: a whole 4x4x16 slice. The times are simulated.
512 devices in a mesh: seq: 64 (over x, z), head: 8 (over y, core).
Axes of the slice: x: 4, y: 4, z: 16, core: 2. Of those that a mesh axis runs over, the one named last changes fastest.
Arguments:
- queries: bfloat16 [24576, 4096], P(('seq', 'head')), may hold values from -5 to 5
- keys: bfloat16 [24576, 4096], P(('seq', 'head')), may hold values from -5 to 5
- values: bfloat16 [24576, 4096], P(('seq', 'head')), may hold values from -6 to 6
- dout: bfloat16 [24576, 4096], P(('seq', 'head')), may hold values from -6 to 6
- selected: int32 [1024, 3], P('seq'), may hold values from 0 to 63, as said below
Outputs:
- attended: bfloat16 [24576, 4096], P('seq', 'head')
- grad_queries: bfloat16 [24576, 4096], P('seq', 'head')
- grad_keys: bfloat16 [24576, 4096], P('seq', 'head')
- grad_values: bfloat16 [24576, 4096], P('seq', 'head')
Inputs may be any that keep to these rules, and one draw needn't show every extreme that they name: `selected`: row g belongs to query block g in key-value block b = g // 16; an entry equal to b marks an unused slot, the other entries of a row are distinct and smaller than b; among the 16 rows of one key-value block no other block is named more than 1 times.
All inputs are finite; a program needn't handle non-finite values.
Results may differ from a plain program's by a relative error of at most 0.014.
The roundings to bfloat16 on the way count: a program that leaves them out, or rounds other values in their place, can miss the bound.
Values may be sent and summed in bfloat16 or wider, within the bound.
A program may use at most 64 MiB of HBM per device.

v0:
```python
import math

import jax
import jax.numpy as jnp
from jax import lax
from jax.sharding import PartitionSpec as P

HD = 128
QB = 24
TOPK = 3
CAP = 1


NEGATIVE = -1e30


def part_forward(query_rows, keys_here, values_here, causal):
    scale = 1.0 / math.sqrt(HD)
    scores = (
        jnp.einsum("rhd,khd->hrk", query_rows, keys_here, preferred_element_type=jnp.float32)
        * scale
    )
    if causal is not None:
        scores = jnp.where(causal[None], scores, NEGATIVE)
    peak = jnp.max(scores, axis=2, keepdims=True)
    log_total = peak + jnp.log(jnp.sum(jnp.exp(scores - peak), axis=2, keepdims=True))
    probs = jnp.exp(scores - log_total).astype(jnp.bfloat16)
    partial_out = jnp.einsum("hrk,khd->rhd", probs, values_here, preferred_element_type=jnp.float32)
    return (partial_out.astype(jnp.bfloat16), log_total[:, :, 0].T)


def part_backward(query_rows, grad_rows, lse_rows, delta_rows, keys_here, values_here, causal):
    scale = 1.0 / math.sqrt(HD)
    scores = (
        jnp.einsum("rhd,khd->hrk", query_rows, keys_here, preferred_element_type=jnp.float32)
        * scale
    )
    if causal is not None:
        scores = jnp.where(causal[None], scores, NEGATIVE)
    probs = jnp.exp(scores - lse_rows.T[:, :, None])
    grad_v = jnp.einsum(
        "hrk,rhd->khd", probs.astype(jnp.bfloat16), grad_rows, preferred_element_type=jnp.float32
    )
    dprobs = jnp.einsum("rhd,khd->hrk", grad_rows, values_here, preferred_element_type=jnp.float32)
    dscores = (probs * (dprobs - delta_rows.T[:, :, None])).astype(jnp.bfloat16)
    grad_q = (
        jnp.einsum("hrk,khd->rhd", dscores, keys_here, preferred_element_type=jnp.float32) * scale
    )
    grad_k = (
        jnp.einsum("hrk,rhd->khd", dscores, query_rows, preferred_element_type=jnp.float32) * scale
    )
    return (grad_q.astype(jnp.bfloat16), grad_k, grad_v)


def local(queries, keys, values, dout, selected):
    q_all, k_all, v_all, g_all = (
        lax.all_to_all(queries, "head", split_axis=1, concat_axis=0, tiled=True),
        lax.all_to_all(keys, "head", split_axis=1, concat_axis=0, tiled=True),
        lax.all_to_all(values, "head", split_axis=1, concat_axis=0, tiled=True),
        lax.all_to_all(dout, "head", split_axis=1, concat_axis=0, tiled=True),
    )
    tokens_here = q_all.shape[0]
    features = q_all.shape[1]
    head_count = features // HD
    block_count = tokens_here // QB
    seq_count = lax.axis_size("seq")
    own_index = lax.axis_index("seq")
    slot_count = seq_count * CAP
    per_block = slot_count
    while per_block % 2 == 0 and per_block // 2 * QB >= 512:
        per_block = per_block // 2
    block_rows = per_block * QB
    row_blocks = slot_count // per_block
    q_three = q_all.reshape(tokens_here, head_count, HD)
    k_three = k_all.reshape(tokens_here, head_count, HD)
    v_three = v_all.reshape(tokens_here, head_count, HD)
    g_three = g_all.reshape(tokens_here, head_count, HD)
    token_ids = jnp.arange(tokens_here, dtype=jnp.int32)
    causal = token_ids[:, None] >= token_ids[None, :]
    owners = selected.reshape(-1)
    active = owners != own_index
    entry_ids = jnp.arange(owners.shape[0], dtype=jnp.int32)
    earlier_same = (
        (owners[:, None] == owners[None, :])
        & active[None, :]
        & (entry_ids[None, :] < entry_ids[:, None])
    )
    ranking = jnp.sum(earlier_same.astype(jnp.int32), axis=1)
    position = jnp.where(active, owners * CAP + ranking, slot_count)
    fetch_at = jnp.minimum(position, slot_count - 1)

    def pack(blocks):
        spread = jnp.repeat(blocks, TOPK, axis=0)
        empty = jnp.zeros((slot_count,) + blocks.shape[1:], blocks.dtype)
        return empty.at[position].set(spread, mode="drop")

    flags = (
        jnp.zeros((slot_count,), jnp.bfloat16)
        .at[position]
        .set(1.0, mode="drop")
        .reshape(seq_count, CAP)
    )
    q_blocks = q_all.reshape(block_count, QB, features)
    g_blocks = g_all.reshape(block_count, QB, features)
    sent_q, got_flags = (
        lax.all_to_all(pack(q_blocks), "seq", split_axis=0, concat_axis=0, tiled=True),
        lax.all_to_all(flags, "seq", split_axis=0, concat_axis=0, tiled=True),
    )
    q_in = sent_q.reshape(row_blocks, block_rows, head_count, HD)
    busy = jnp.max(got_flags.reshape(row_blocks, per_block).astype(jnp.float32), axis=1) > 0.0

    def run_forward(block_q):
        return part_forward(block_q, k_three, v_three, None)

    def forward_block(inputs):
        block_q, block_busy = inputs
        return run_forward(block_q)

    part_out, part_lse = lax.map(forward_block, (q_in, busy))
    own_out, own_lse = part_forward(q_three, k_three, v_three, causal)
    back_out = lax.all_to_all(
        part_out.reshape(seq_count, CAP * QB, features),
        "seq",
        split_axis=0,
        concat_axis=0,
        tiled=True,
    )
    back_lse = lax.all_to_all(
        part_lse.reshape(seq_count, CAP * QB, head_count),
        "seq",
        split_axis=0,
        concat_axis=0,
        tiled=True,
    )
    far_out = back_out.reshape(slot_count, QB, head_count, HD)[fetch_at].astype(jnp.float32)
    far_out = far_out.reshape(block_count, TOPK, QB, head_count, HD)
    far_lse = jnp.where(active[:, None, None], back_lse[fetch_at], NEGATIVE)
    far_lse = far_lse.reshape(block_count, TOPK, QB, head_count)
    all_out = jnp.concatenate(
        [own_out.astype(jnp.float32).reshape(block_count, 1, QB, head_count, HD), far_out], axis=1
    )
    all_lse = jnp.concatenate([own_lse.reshape(block_count, 1, QB, head_count), far_lse], axis=1)
    lse_peak = jnp.max(all_lse, axis=1, keepdims=True)
    log_total = lse_peak + jnp.log(jnp.sum(jnp.exp(all_lse - lse_peak), axis=1, keepdims=True))
    weights = jnp.exp(all_lse - log_total)
    attended = jnp.sum(weights[..., None] * all_out, axis=1).astype(jnp.bfloat16)
    lse_blocks = log_total[:, 0]
    delta_blocks = jnp.sum(
        g_all.reshape(block_count, QB, head_count, HD).astype(jnp.float32)
        * attended.astype(jnp.float32),
        axis=3,
    )
    got_lse, got_delta = (
        lax.all_to_all(pack(lse_blocks), "seq", split_axis=0, concat_axis=0, tiled=True),
        lax.all_to_all(pack(delta_blocks), "seq", split_axis=0, concat_axis=0, tiled=True),
    )
    sent_g = lax.all_to_all(pack(g_blocks), "seq", split_axis=0, concat_axis=0, tiled=True)
    g_in = sent_g.reshape(row_blocks, block_rows, head_count, HD)
    lse_in = got_lse.reshape(row_blocks, block_rows, head_count)
    delta_in = got_delta.reshape(row_blocks, block_rows, head_count)
    own_dq, own_dk, own_dv = part_backward(
        q_three,
        g_three,
        lse_blocks.reshape(tokens_here, head_count),
        delta_blocks.reshape(tokens_here, head_count),
        k_three,
        v_three,
        causal,
    )

    def backward_block(carry, inputs):
        block_q, block_g, block_lse, block_delta, block_busy = inputs
        part_dq, part_dk, part_dv = part_backward(
            block_q, block_g, block_lse, block_delta, k_three, v_three, None
        )
        return ((carry[0] + part_dk, carry[1] + part_dv), part_dq)

    (grad_k, grad_v), part_dq = lax.scan(
        backward_block, (own_dk, own_dv), (q_in, g_in, lse_in, delta_in, busy)
    )
    back_dq = lax.all_to_all(
        part_dq.reshape(seq_count, CAP * QB, features),
        "seq",
        split_axis=0,
        concat_axis=0,
        tiled=True,
    )
    far_dq = back_dq.reshape(slot_count, QB, head_count, HD)[fetch_at].astype(jnp.float32)
    far_dq = jnp.where(active[:, None, None, None], far_dq, 0.0).reshape(
        block_count, TOPK, QB, head_count, HD
    )
    grad_q = own_dq.astype(jnp.float32).reshape(block_count, QB, head_count, HD) + jnp.sum(
        far_dq, axis=1
    )
    return (
        attended.reshape(tokens_here, features),
        grad_q.astype(jnp.bfloat16).reshape(tokens_here, features),
        grad_k.astype(jnp.bfloat16).reshape(tokens_here, features),
        grad_v.astype(jnp.bfloat16).reshape(tokens_here, features),
    )


def solution(mesh):
    placed = (
        P(("seq", "head"), None),
        P(("seq", "head"), None),
        P(("seq", "head"), None),
        P(("seq", "head"), None),
        P("seq", None),
    )
    return jax.shard_map(
        local,
        mesh=mesh,
        in_specs=placed,
        out_specs=(P("seq", "head"), P("seq", "head"), P("seq", "head"), P("seq", "head")),
        check_vma=False,
    )
```

profile of v0, /device:TPU:14, one launch (start us, length us, event | category | flops | bytes accessed | tf_op | source)
XLA Modules:
  0.0 529.5 jit_solution(121553264007561912)
XLA Ops:
  2.5 4.9 all-to-all-start
  9.2 5.7 %all-to-all-done = bf16[48,8,512]{2,0,1:T(8,128)(2,1)S(1)} async-done(((bf16[48,8,512]{2,0,1:T(8,128)(2,1)}), bf16[48,8,512]{2,0,1:T(8,128)(2,1)S(1)}, u32[]{:S(2)}, u32[]{:S(2)}) %all-to-all-start) | async-done | bytes 393248 | tf_op jit(solution)/shard_map/all_to_all | solution.py:57
  14.9 4.8 all-to-all-start.1
  21.0 6.3 %all-to-all-done.1 = bf16[48,8,512]{2,0,1:T(8,128)(2,1)S(1)} async-done(((bf16[48,8,512]{2,0,1:T(8,128)(2,1)}), bf16[48,8,512]{2,0,1:T(8,128)(2,1)S(1)}, u32[]{:S(2)}, u32[]{:S(2)}) %all-to-all-start.1) | async-done | bytes 393248 | tf_op jit(solution)/shard_map/all_to_all | solution.py:58
  27.2 4.8 all-to-all-start.3
  33.9 6.5 %scatter_fusion = bf16[64,24,512]{2,1,0:T(8,128)(2,1)} fusion(bf16[64,24,512]{2,1,0:T(8,128)(2,1)} %broadcast.132.clone, s32[48]{0:T(128)S(1)} %fusion.46, bf16[48,24,512]{2,1,0:T(8,128)(2,1)S(1)} %bitcast.188), kind=kCustom, calls=%fused_computation.3 | custom fusion | bytes 3539136 | tf_op jit(solution)/shard_map/scatter | solution.py:95
  40.4 19.2 %all-to-all-start.2 = ((bf16[64,24,512]{2,1,0:T(8,128)(2,1)}), bf16[64,24,512]{2,1,0:T(8,128)(2,1)S(1)}, u32[]{:S(2)}, u32[]{:S(2)}) async-start(bf16[64,24,512]{2,1,0:T(8,128)(2,1)} %scatter_fusion), calls=%async_computation.2 | async-start | bytes 3145728 | tf_op jit(solution)/shard_map/all_to_all | solution.py:106
  61.4 73.9 %all-to-all-done.2 = bf16[64,24,512]{2,1,0:T(8,128)(2,1)S(1)} async-done(((bf16[64,24,512]{2,1,0:T(8,128)(2,1)}), bf16[64,24,512]{2,1,0:T(8,128)(2,1)S(1)}, u32[]{:S(2)}, u32[]{:S(2)}) %all-to-all-start.2) | async-done | bytes 1572896 | tf_op jit(solution)/shard_map/all_to_all | solution.py:106
  135.3 4.8 all-to-all-start.6
  145.2 11.5 %while.26 = (s32[]{:T(128)}, bf16[2,768,4,128]{3,2,1,0:T(4,128)(2,1)}, f32[2,768,4]{1,0,2:T(2,128)}, bf16[2,768,4,128]{3,1,2,0:T(8,128)(2,1)S(1)}, bf16[384,4,12...) while((s32[]{:T(128)}, bf16[2,768,4,128]{3,2,1,0:T(4,128)(2,1)}, ...), condition=%wide.region_7.8_spmd, body=%wide.region_4.7_spmd.sunk | while | flops 613807104 | bytes 18223208 | solution.py:119
  158.3 7.7 %all-to-all-start.4 = ((f32[64,24,4]{1,2,0:T(4,128)}), f32[64,24,4]{1,2,0:T(4,128)S(1)}, u32[]{:S(2)}, u32[]{:S(2)}) async-start(f32[64,24,4]{1,2,0:T(4,128)} %copy.243), calls=%async_computation.4 | async-start | bytes 262144 | tf_op jit(solution)/shard_map/all_to_all | solution.py:128
  169.4 7.3 %scatter_fusion.2 = bf16[64,24,512]{2,1,0:T(8,128)(2,1)} fusion(bf16[64,24,512]{2,1,0:T(8,128)(2,1)} %broadcast.132.clone.1, s32[48]{0:T(128)S(1)} %copy-done.26, bf16[48,24,512]{2,1,0:T(8,128)(2,1)} %bitcast.189), kind=kCustom, calls=%fused_computation.5 | custom fusion | bytes 3539136 | tf_op jit(solution)/shard_map/scatter | solution.py:95
  176.7 5.2 all-to-all-done.4
  181.9 10.4 %all-to-all-start.8 = ((bf16[64,24,512]{2,1,0:T(8,128)(2,1)}), bf16[64,24,512]{2,1,0:T(8,128)(2,1)}, u32[]{:S(2)}, u32[]{:S(2)}) async-start(bf16[64,24,512]{2,1,0:T(8,128)(2,1)} %scatter_fusion.2), calls=%async_computation.8 | async-start | bytes 3145728 | tf_op jit(solution)/shard_map/all_to_all | solution.py:157
  200.7 5.3 %scatter_fusion.1 = f32[64,24,4]{1,2,0:T(4,128)} fusion(f32[64,24,4]{1,2,0:T(4,128)} %broadcast.135.clone, s32[48]{0:T(128)S(1)} %copy-done.27, f32[48,24,4]{1,2,0:T(4,128)S(1)} %bitcast.185), kind=kCustom, calls=%fused_computation.4 | custom fusion | bytes 55488 | tf_op jit(solution)/shard_map/scatter | solution.py:95
  206.0 62.0 %all-to-all-done.8 = bf16[64,24,512]{2,1,0:T(8,128)(2,1)} async-done(((bf16[64,24,512]{2,1,0:T(8,128)(2,1)}), bf16[64,24,512]{2,1,0:T(8,128)(2,1)}, u32[]{:S(2)}, u32[]{:S(2)}) %all-to-all-start.8) | async-done | bytes 1572896 | tf_op jit(solution)/shard_map/all_to_all | solution.py:157
  268.1 6.9 %all-to-all-start.7 = ((f32[64,24,4]{1,2,0:T(4,128)}), f32[64,24,4]{1,2,0:T(4,128)S(1)}, u32[]{:S(2)}, u32[]{:S(2)}) async-start(f32[64,24,4]{1,2,0:T(4,128)} %scatter_fusion.1), calls=%async_computation.7 | async-start | bytes 262144 | tf_op jit(solution)/shard_map/all_to_all | solution.py:154
  275.0 3.6 reshape.293
  278.6 11.8 %all-to-all-done.7 = f32[64,24,4]{1,2,0:T(4,128)S(1)} async-done(((f32[64,24,4]{1,2,0:T(4,128)}), f32[64,24,4]{1,2,0:T(4,128)S(1)}, u32[]{:S(2)}, u32[]{:S(2)}) %all-to-all-start.7) | async-done | bytes 24608 | tf_op jit(solution)/shard_map/all_to_all | solution.py:154
  290.5 6.6 %all-to-all-start.5 = ((bf16[64,24,512]{2,1,0:T(8,128)(2,1)}), bf16[64,24,512]{2,1,0:T(8,128)(2,1)}, u32[]{:S(2)}, u32[]{:S(2)}) async-start(bf16[64,24,512]{2,1,0:T(8,128)(2,1)} %reshape.293), calls=%async_computation.5 | async-start | bytes 3145728 | tf_op jit(solution)/shard_map/all_to_all | solution.py:121
  305.8 3.5 reshape.303
  317.0 55.9 %all-to-all-done.5 = bf16[64,24,512]{2,1,0:T(8,128)(2,1)} async-done(((bf16[64,24,512]{2,1,0:T(8,128)(2,1)}), bf16[64,24,512]{2,1,0:T(8,128)(2,1)}, u32[]{:S(2)}, u32[]{:S(2)}) %all-to-all-start.5) | async-done | bytes 1572896 | tf_op jit(solution)/shard_map/all_to_all | solution.py:121
  372.8 3.5 reshape.294
  376.3 4.2 gather_fusion.1
  380.5 3.9 multiply_reduce_fusion.1
  386.7 5.3 %scatter_fusion.3 = f32[64,24,4]{1,2,0:T(4,128)} fusion(f32[64,24,4]{1,2,0:T(4,128)} %broadcast.135.clone.1, s32[48]{0:T(128)S(1)} %copy-done.27, f32[48,24,4]{1,2,0:T(4,128)S(1)} %bitcast.184), kind=kCustom, calls=%fused_computation.6 | custom fusion | bytes 55488 | tf_op jit(solution)/shard_map/scatter | solution.py:95
  392.0 7.2 %all-to-all-start.9 = ((f32[64,24,4]{1,2,0:T(4,128)}), f32[64,24,4]{1,2,0:T(4,128)}, u32[]{:S(2)}, u32[]{:S(2)}) async-start(f32[64,24,4]{1,2,0:T(4,128)} %scatter_fusion.3), calls=%async_computation.9 | async-start | bytes 262144 | tf_op jit(solution)/shard_map/all_to_all | solution.py:155
  403.2 11.2 %all-to-all-done.9 = f32[64,24,4]{1,2,0:T(4,128)} async-done(((f32[64,24,4]{1,2,0:T(4,128)}), f32[64,24,4]{1,2,0:T(4,128)}, u32[]{:S(2)}, u32[]{:S(2)}) %all-to-all-start.9) | async-done | bytes 24608 | tf_op jit(solution)/shard_map/all_to_all | solution.py:155
  417.0 20.5 %while.27 = (s32[]{:T(128)}, f32[384,4,128]{0,2,1:T(8,128)S(1)}, f32[384,4,128]{0,2,1:T(8,128)}, bf16[2,768,4,128]{3,2,1,0:T(4,128)(2,1)}, bf16[2,768,4,128]{3,1...) while((s32[]{:T(128)}, f32[384,4,128]{0,2,1:T(8,128)S(1)}, ...), condition=%wide.region_16.17_spmd, body=%wide.region_15.16_spmd.sunk | while | flops 1520762880 | bytes 51646712 | solution.py:178
  437.5 3.6 reshape.306
  441.2 6.8 %all-to-all-start.10 = ((bf16[64,24,512]{2,1,0:T(8,128)(2,1)}), bf16[64,24,512]{2,1,0:T(8,128)(2,1)}, u32[]{:S(2)}, u32[]{:S(2)}) async-start(bf16[64,24,512]{2,1,0:T(8,128)(2,1)} %reshape.306), calls=%async_computation.10 | async-start | bytes 3145728 | tf_op jit(solution)/shard_map/all_to_all | solution.py:181
  453.6 70.0 %all-to-all-done.10 = bf16[64,24,512]{2,1,0:T(8,128)(2,1)} async-done(((bf16[64,24,512]{2,1,0:T(8,128)(2,1)}), bf16[64,24,512]{2,1,0:T(8,128)(2,1)}, u32[]{:S(2)}, u32[]{:S(2)}) %all-to-all-start.10) | async-done | bytes 1572896 | tf_op jit(solution)/shard_map/all_to_all | solution.py:181
  (182 shorter events, 95.3 us)
Async XLA Ops:
  0.6 19.1 %copy-start.24 = (s32[16,3]{0,1:T(4,128)S(1)}, s32[16,3]{0,1:T(4,128)}, u32[]{:S(2)}) copy-start(s32[16,3]{0,1:T(4,128)} %param.13) | copy-start | bytes 580
  0.6 19.3 %copy-start.18 = (bf16[48,4096]{1,0:T(8,128)(2,1)S(1)}, bf16[48,4096]{1,0:T(8,128)(2,1)}, u32[]{:S(2)}) copy-start(bf16[48,4096]{1,0:T(8,128)(2,1)} %param.11) | copy-start | bytes 1179652
  2.5 12.4 %all-to-all-start = ((bf16[48,8,512]{2,0,1:T(8,128)(2,1)}), bf16[48,8,512]{2,0,1:T(8,128)(2,1)S(1)}, u32[]{:S(2)}, u32[]{:S(2)}) async-start(bf16[48,8,512]{2,0,1:T(8,128)(2,1)} %bitcast.136), calls=%async_computation | async-start | bytes 786432 | tf_op jit(solution)/shard_map/all_to_all | solution.py:57
  14.9 19.1 %copy-start.11 = (bf16[48,8,512]{2,0,1:T(8,128)(2,1)}, bf16[48,8,512]{2,0,1:T(8,128)(2,1)S(1)}, u32[]{:S(2)}) copy-start(bf16[48,8,512]{2,0,1:T(8,128)(2,1)S(1)} %all-to-all-done) | copy-start | bytes 1179652
  14.9 12.3 %all-to-all-start.1 = ((bf16[48,8,512]{2,0,1:T(8,128)(2,1)}), bf16[48,8,512]{2,0,1:T(8,128)(2,1)S(1)}, u32[]{:S(2)}, u32[]{:S(2)}) async-start(bf16[48,8,512]{2,0,1:T(8,128)(2,1)} %bitcast.135), calls=%async_computation.1 | async-start | bytes 786432 | tf_op jit(solution)/shard_map/all_to_all | solution.py:58
  27.2 13.2 %all-to-all-start.3 = ((bf16[48,8,512]{2,0,1:T(8,128)(2,1)}), bf16[48,8,512]{2,0,1:T(8,128)(2,1)S(1)}, u32[]{:S(2)}, u32[]{:S(2)}) async-start(bf16[48,8,512]{2,0,1:T(8,128)(2,1)} %bitcast.134), calls=%async_computation.3 | async-start | bytes 786432 | tf_op jit(solution)/shard_map/all_to_all | solution.py:59
  32.6 7.8 %copy-start.25 = (s32[48]{0:T(128)}, s32[48]{0:T(128)S(1)}, u32[]{:S(2)}) copy-start(s32[48]{0:T(128)S(1)} %fusion.46) | copy-start | bytes 580
  40.4 19.2 %copy-start.19 = (bf16[48,4096]{1,0:T(8,128)(2,1)S(1)}, bf16[48,4096]{1,0:T(8,128)(2,1)}, u32[]{:S(2)}) copy-start(bf16[48,4096]{1,0:T(8,128)(2,1)} %param.12) | copy-start | bytes 1179652
  40.4 94.9 %all-to-all-start.2 = ((bf16[64,24,512]{2,1,0:T(8,128)(2,1)}), bf16[64,24,512]{2,1,0:T(8,128)(2,1)S(1)}, u32[]{:S(2)}, u32[]{:S(2)}) async-start(bf16[64,24,512]{2,1,0:T(8,128)(2,1)} %scatter_fusion), calls=%async_computation.2 | async-start | bytes 3145728 | tf_op jit(solution)/shard_map/all_to_all | solution.py:106
  135.3 23.0 %all-to-all-start.6 = ((bf16[48,8,512]{2,0,1:T(8,128)(2,1)}), bf16[48,8,512]{2,0,1:T(8,128)(2,1)}, u32[]{:S(2)}, u32[]{:S(2)}) async-start(bf16[48,8,512]{2,0,1:T(8,128)(2,1)} %bitcast.133), calls=%async_computation.6 | async-start | bytes 786432 | tf_op jit(solution)/shard_map/all_to_all | solution.py:60
  156.7 12.7 %copy-start.26 = (s32[48]{0:T(128)S(1)}, s32[48]{0:T(128)}, u32[]{:S(2)}) copy-start(s32[48]{0:T(128)} %copy-done.25) | copy-start | bytes 580
  158.3 23.6 %all-to-all-start.4 = ((f32[64,24,4]{1,2,0:T(4,128)}), f32[64,24,4]{1,2,0:T(4,128)S(1)}, u32[]{:S(2)}, u32[]{:S(2)}) async-start(f32[64,24,4]{1,2,0:T(4,128)} %copy.243), calls=%async_computation.4 | async-start | bytes 262144 | tf_op jit(solution)/shard_map/all_to_all | solution.py:128
  176.7 15.7 %copy-start.28 = (s32[48]{0:T(128)S(1)}, s32[48]{0:T(128)}, u32[]{:S(2)}) copy-start(s32[48]{0:T(128)} %get-tuple-element.220) | copy-start | bytes 580
  176.7 18.1 %copy-start.9 = (bf16[384,4,128]{2,1,0:T(4,128)(2,1)S(1)}, bf16[384,4,128]{2,1,0:T(4,128)(2,1)}, u32[]{:S(2)}) copy-start(bf16[384,4,128]{2,1,0:T(4,128)(2,1)} %copy-done.8) | copy-start | bytes 1179652
  181.9 86.2 %all-to-all-start.8 = ((bf16[64,24,512]{2,1,0:T(8,128)(2,1)}), bf16[64,24,512]{2,1,0:T(8,128)(2,1)}, u32[]{:S(2)}, u32[]{:S(2)}) async-start(bf16[64,24,512]{2,1,0:T(8,128)(2,1)} %scatter_fusion.2), calls=%async_computation.8 | async-start | bytes 3145728 | tf_op jit(solution)/shard_map/all_to_all | solution.py:157
  196.4 4.3 copy-start.27
  200.0 68.0 %copy-start.21 = (f32[8,24,8]{1,2,0:T(8,128)}, f32[8,24,8]{1,2,0:T(8,128)S(1)}, u32[]{:S(2)}) copy-start(f32[8,24,8]{1,2,0:T(8,128)S(1)} %get-tuple-element.247) | copy-start | bytes 18436
  268.1 22.4 %all-to-all-start.7 = ((f32[64,24,4]{1,2,0:T(4,128)}), f32[64,24,4]{1,2,0:T(4,128)S(1)}, u32[]{:S(2)}, u32[]{:S(2)}) async-start(f32[64,24,4]{1,2,0:T(4,128)} %scatter_fusion.1), calls=%async_computation.7 | async-start | bytes 262144 | tf_op jit(solution)/shard_map/all_to_all | solution.py:154
  290.5 9.7 %copy-start.16 = (f32[64,24,4]{1,2,0:T(4,128)}, f32[64,24,4]{1,2,0:T(4,128)S(1)}, u32[]{:S(2)}) copy-start(f32[64,24,4]{1,2,0:T(4,128)S(1)} %all-to-all-done.7) | copy-start | bytes 73732
  290.5 82.4 %all-to-all-start.5 = ((bf16[64,24,512]{2,1,0:T(8,128)(2,1)}), bf16[64,24,512]{2,1,0:T(8,128)(2,1)}, u32[]{:S(2)}, u32[]{:S(2)}) async-start(bf16[64,24,512]{2,1,0:T(8,128)(2,1)} %reshape.293), calls=%async_computation.5 | async-start | bytes 3145728 | tf_op jit(solution)/shard_map/all_to_all | solution.py:121
  304.7 4.7 copy-start.23
  304.7 4.8 copy-start.22
  310.9 5.3 %copy-start.17 = (f32[64,24,4]{1,2,0:T(4,128)S(1)}, f32[64,24,4]{1,2,0:T(4,128)}, u32[]{:S(2)}) copy-start(f32[64,24,4]{1,2,0:T(4,128)} %copy-done.16) | copy-start | bytes 73732
  380.5 4.7 copy-start.14
  392.0 22.4 %all-to-all-start.9 = ((f32[64,24,4]{1,2,0:T(4,128)}), f32[64,24,4]{1,2,0:T(4,128)}, u32[]{:S(2)}, u32[]{:S(2)}) async-start(f32[64,24,4]{1,2,0:T(4,128)} %scatter_fusion.3), calls=%async_computation.9 | async-start | bytes 262144 | tf_op jit(solution)/shard_map/all_to_all | solution.py:155
  399.2 3.4 copy-start.15
  402.6 14.4 %copy-start.20 = (f32[2,768,4]{1,0,2:T(2,128)S(1)}, f32[2,768,4]{1,0,2:T(2,128)}, u32[]{:S(2)}) copy-start(f32[2,768,4]{1,0,2:T(2,128)} %reshape.300) | copy-start | bytes 73732
  441.2 6.8 %copy-start.13 = (bf16[16,24,4,128]{3,2,1,0:T(4,128)(2,1)S(1)}, bf16[16,24,4,128]{3,2,1,0:T(4,128)(2,1)}, u32[]{:S(2)}) copy-start(bf16[16,24,4,128]{3,2,1,0:T(4,128)(2,1)} %copy-done.12) | copy-start | bytes 1179652
  441.2 7.6 %copy-start.5 = (bf16[4,384,384]{1,2,0:T(8,128)(2,1)S(1)}, bf16[4,384,384]{1,2,0:T(8,128)(2,1)}, u32[]{:S(2)}) copy-start(bf16[4,384,384]{1,2,0:T(8,128)(2,1)} %copy-done.4) | copy-start | bytes 3538948
  441.2 7.6 %copy-start.10 = (bf16[384,4,128]{2,1,0:T(4,128)(2,1)S(1)}, bf16[384,4,128]{2,1,0:T(4,128)(2,1)}, u32[]{:S(2)}) copy-start(bf16[384,4,128]{2,1,0:T(4,128)(2,1)} %copy-done.8) | copy-start | bytes 1179652
  441.2 82.5 %all-to-all-start.10 = ((bf16[64,24,512]{2,1,0:T(8,128)(2,1)}), bf16[64,24,512]{2,1,0:T(8,128)(2,1)}, u32[]{:S(2)}, u32[]{:S(2)}) async-start(bf16[64,24,512]{2,1,0:T(8,128)(2,1)} %reshape.306), calls=%async_computation.10 | async-start | bytes 3145728 | tf_op jit(solution)/shard_map/all_to_all | solution.py:181
  450.2 2.5 copy-start.2
  (12 other events, 14.9 us)
where the time goes:
time: 533 us; the launch traced here: 530 us
  waiting for transfers between devices  302 us (57%)
  local copies, waits for them, and re-layouts  102 us (19%)
  starting transfers between devices  84.1 us (16%)
  matrix products  27.1 us (5%)
  other arithmetic  12.6 us (2%)
    all_to_all x1, waiting for transfers between devices, local(): lax.all_to_all(pack(q_blocks), 'seq', split_axis=0, concat_axis=0, tiled=...  73.9 us
    all_to_all x1, waiting for transfers between devices, local(): lax.all_to_all(part_dq.reshape(seq_count, CAP * QB, features), 'seq', spl...  70 us
    all_to_all x1, waiting for transfers between devices, local(): lax.all_to_all(pack(g_blocks), 'seq', split_axis=0, concat_axis=0, tiled=...  62 us
    all_to_all x1, waiting for transfers between devices, local(): lax.all_to_all(part_out.reshape(seq_count, CAP * QB, features), 'seq', sp...  55.9 us
    scatter x4, local copies, waits for them, and re-layouts, pack(): return empty.at[position].set(spread, mode='drop')  24.4 us
    all_to_all x1, starting transfers between devices, local(): lax.all_to_all(pack(q_blocks), 'seq', split_axis=0, concat_axis=0, tiled=...  19.2 us
    all_to_all x1, waiting for transfers between devices, local(): lax.all_to_all(pack(lse_blocks), 'seq', split_axis=0, concat_axis=0, tile...  11.8 us
    all_to_all x1, waiting for transfers between devices, local(): lax.all_to_all(pack(delta_blocks), 'seq', split_axis=0, concat_axis=0, ti...  11.2 us
  transfers between devices with their start and end apart: 11, of which 9 were waited for; matrix products, arithmetic and copies ran while one was open for 16% of the time, Pallas kernels for 0%

commit v1 on v0

v1 whole, which is shorter than its diff:
```python
import functools
import math

import jax
import jax.numpy as jnp
import numpy as np
from jax import lax
from jax.experimental import pallas as pl
from jax.experimental.pallas import tpu as pltpu
from jax.sharding import PartitionSpec as P

HD = 128
QB = 24
TOPK = 3
ZN = 16
NEGATIVE = -1e30
MESH = pl.DeviceIdType.MESH
BF = jnp.bfloat16
F32 = jnp.float32
VMEM_LIMIT = 60 * 1024 * 1024


def dot(a, b, ca, cb):
    return lax.dot_general(a, b, (((ca,), (cb,)), ((), ())), preferred_element_type=F32)


def split3(a):
    high = a.astype(BF)
    rest = a - high.astype(F32)
    mid = rest.astype(BF)
    low = (rest - mid.astype(F32)).astype(BF)
    return jnp.concatenate([high, mid, low], axis=0)


def loop(start, stop, body):
    def step(index, carry):
        body(index)
        return carry

    lax.fori_loop(start, stop, step, 0)


def kernel(
    xn, zn, hn, heads,
    sel, inv, flag, spread, owner_mask, q_in, k_in, v_in, g_in,
    att, gq, gk, gv,
    qa, ka, va, ga, qf, gf, kh, vh, kt, vt,
    pk, r1, f, rt, r2, g0, g1, g2, g3, su, srx, s0, s1, ws, wrz, wr,
    qc, gc, pb, db, li, sv, wv, dk, dv, aj, lr, dr, fo,
    ssem, rsem, lsem,
):
    scale = 1.0 / math.sqrt(HD)
    seq = lax.axis_index("seq")
    head = lax.axis_index("head")
    x = lax.div(seq, zn)
    z = lax.rem(seq, zn)
    rows = q_in.shape[0]
    width = heads * HD
    tokens = qa.shape[0]
    far = zn * QB

    def z_partner(k):
        half = lax.div(k + 1, 2)
        return lax.rem(z + jnp.where(lax.rem(k, 2) == 1, half, zn - half), zn)

    def z_send(src, dst, lower, down, flow):
        def body(k):
            zi = z_partner(k)
            own = jnp.where(zi < z, 1, 0) if down else jnp.where(zi > z, 1, 0)
            start = 0 if lower else x + 1 - own
            count = x + own if lower else xn - 1 - x + own
            for m in range(1, xn + 1):

                @pl.when(count == m)
                def _():
                    pltpu.make_async_remote_copy(
                        src_ref=src.at[pl.ds(start, m), zi],
                        dst_ref=dst.at[pl.ds(start, m), z],
                        send_sem=ssem.at[flow, zi],
                        recv_sem=rsem.at[flow, z],
                        device_id={"seq": x * zn + zi},
                        device_id_type=MESH,
                    ).start()

        loop(1, zn, body)

    def z_wait(buf, lower, down, sem, sent):
        base = x if lower else xn - 1 - x

        def body(k):
            zi = z_partner(k)
            below = jnp.where(zi < z, 1, 0)
            count = base + (below if down == sent else 1 - below)
            for m in range(1, xn + 1):

                @pl.when(count == m)
                def _():
                    part = buf.at[0, pl.ds(0, m)]
                    pltpu.make_async_copy(part, part, sem.at[zi]).wait()

        loop(1, zn, body)

    def x_send(src, dst, down, flow):
        def body(xi):
            pltpu.make_async_remote_copy(
                src_ref=src.at[xi],
                dst_ref=dst.at[x],
                send_sem=ssem.at[flow, xi],
                recv_sem=rsem.at[flow, x],
                device_id={"seq": xi * zn + z},
                device_id_type=MESH,
            ).start()

        if down:
            loop(0, x, body)
        else:
            loop(x + 1, xn, body)

    def x_wait(buf, down, sem, sent):
        whole = buf.at[0]
        body = lambda xi: pltpu.make_async_copy(whole, whole, sem.at[xi]).wait()
        if down == sent:
            loop(0, x, body)
        else:
            loop(x + 1, xn, body)

    def keep(dst, src, index):
        dst[index] = src[index]

    def down_first(src, mid, zf, flow):
        if zf:
            loop(0, xn, lambda i: keep(mid, src, (i, z)))
            z_send(src, mid, True, True, flow)
        else:
            loop(0, zn, lambda i: keep(mid, src, (x, i)))
            x_send(src, mid, True, flow)

    def down_second(mid, dst, zf, flow):
        if zf:
            z_wait(mid, True, True, rsem.at[flow], False)
            x_send(mid, dst, True, flow + 1)
        else:
            x_wait(mid, True, rsem.at[flow], False)
            z_send(mid, dst, False, True, flow + 1)

    def down_done(mid, dst, zf, flow):
        if zf:
            loop(z + 1, zn, lambda i: keep(dst, mid, (x, i)))
            x_wait(dst, True, rsem.at[flow + 1], False)
        else:
            loop(x + 1, xn, lambda i: keep(dst, mid, (i, z)))
            z_wait(dst, False, True, rsem.at[flow + 1], False)

    def up_first(src, mid, zf, flow):
        if zf:
            loop(0, zn, lambda i: keep(mid, src, (x, i)))
            x_send(src, mid, False, flow)
        else:
            loop(x + 1, xn, lambda i: keep(mid, src, (i, z)))
            z_send(src, mid, False, False, flow)

    def up_second(mid, dst, zf, flow):
        if zf:
            x_wait(mid, False, rsem.at[flow], False)
            z_send(mid, dst, True, False, flow + 1)
        else:
            z_wait(mid, False, False, rsem.at[flow], False)
            x_send(mid, dst, False, flow + 1)

    def up_done(mid, dst, zf, flow):
        if zf:
            loop(0, x, lambda i: keep(dst, mid, (i, z)))
            z_wait(dst, True, False, rsem.at[flow + 1], False)
        else:
            loop(0, z, lambda i: keep(dst, mid, (x, i)))
            x_wait(dst, False, rsem.at[flow + 1], False)

    def drain(buf, zf, flow, down):
        first_z = zf if down else not zf
        z_flow = flow if first_z else flow + 1
        x_flow = flow + 1 if first_z else flow
        z_wait(buf, zf, down, ssem.at[z_flow], True)
        x_wait(buf, down, ssem.at[x_flow], True)

    gg, sr = (g0, g1, g2, g3), (s0, s1)
    zfirst = [h % 2 == 0 for h in range(heads)]
    flow_down = [4 * h for h in range(heads)]
    flow_up = [4 * h + 2 for h in range(heads)]
    flow_stat = [4 * heads + 4 * s for s in range(heads // 2)]
    flow_head = 4 * heads + 4 * (heads // 2)

    f[...] = jnp.zeros_like(f)
    wr[...] = jnp.zeros_like(wr)
    for part in sr:
        part[...] = jnp.zeros_like(part)

    barrier = pltpu.get_barrier_semaphore()

    def greet(target):
        pl.semaphore_signal(barrier, inc=1, device_id=target, device_id_type=MESH)

    loop(1, hn, lambda i: greet({"head": lax.rem(head + i, hn)}))
    loop(1, zn, lambda i: greet({"seq": x * zn + lax.rem(z + i, zn)}))
    loop(1, xn, lambda i: greet({"seq": lax.rem(x + i, xn) * zn + z}))
    pl.semaphore_wait(barrier, hn + zn + xn - 3)

    inputs = ((q_in, qa), (g_in, ga), (k_in, ka), (v_in, va))
    here = pl.ds(pl.multiple_of(head * rows, rows), rows)

    for n, (src, dst) in enumerate(inputs):

        def fan(i, src=src, dst=dst, n=n):
            hi = lax.rem(head + i, hn)
            pltpu.make_async_remote_copy(
                src_ref=src.at[:, pl.ds(pl.multiple_of(hi * width, width), width)],
                dst_ref=dst.at[here],
                send_sem=ssem.at[flow_head + n, hi],
                recv_sem=rsem.at[flow_head + n, head],
                device_id={"head": hi},
                device_id_type=MESH,
            ).start()

        loop(1, hn, fan)
        pltpu.make_async_copy(
            src.at[:, pl.ds(pl.multiple_of(head * width, width), width)], dst.at[here], lsem.at[n]
        ).start()

    def head_wait(dst, sem):
        part = dst.at[pl.ds(0, rows)]

        def body(i):
            pltpu.make_async_copy(part, part, sem.at[lax.rem(head + i, hn)]).wait()

        loop(1, hn, body)

    def arrive(n):
        src, dst = inputs[n]
        pltpu.make_async_copy(
            src.at[:, pl.ds(pl.multiple_of(head * width, width), width)], dst.at[here], lsem.at[n]
        ).wait()
        head_wait(dst, rsem.at[flow_head + n])

    arrive(0)
    qf[...] = qa[...].astype(F32).reshape(qf.shape)
    arrive(1)
    gf[...] = ga[...].astype(F32).reshape(gf.shape)

    def block_of(i, h):
        cols = slice(h * HD, (h + 1) * HD)
        return jnp.concatenate([qf[i, :, cols], gf[i, :, cols]], axis=0).astype(BF)

    def pack(stage):
        def body(zd):
            for h in (2 * stage, 2 * stage + 1):
                f[h, xn, zd] = block_of(zd, h)
            for xd in range(xn):
                i = inv[xd * zn + zd]
                for h in (2 * stage, 2 * stage + 1):
                    pk[h, xd, zd] = block_of(i, h)

        loop(0, zn, body)
        for h in (2 * stage, 2 * stage + 1):
            down_first(pk.at[h], r1.at[h], zfirst[h], flow_down[h])

    def forward_relay(h):
        down_second(r1.at[h], f.at[h], zfirst[h], flow_down[h])

    def scores(stage):
        u = lax.broadcasted_iota(jnp.int32, (tokens, far), 0)
        t = lax.broadcasted_iota(jnp.int32, (tokens, far), 1)

        def body(step):
            hh = lax.rem(step, 2)
            group = x + lax.div(step, 2)
            h = 2 * stage + hh
            both = f[h, group].astype(F32)
            qv = both[:, :QB].reshape(far, HD).astype(BF)
            gv_ = both[:, QB:].reshape(far, HD).astype(BF)
            qc[hh, group] = qv
            gc[hh, group] = gv_
            s = dot(kh[h], qv, 1, 1)
            dp = dot(vh[h], gv_, 1, 1)
            s = jnp.where(u <= t + jnp.where(group == xn, 0, tokens), s, NEGATIVE)
            peak = jnp.max(s, axis=0, keepdims=True)
            p = jnp.exp((s - peak) * scale)
            total = jnp.sum(p, axis=0, keepdims=True)
            pb[hh, group] = p
            db[hh, group] = dp
            inverse = 1.0 / total
            li[hh, group] = inverse
            sv[group, hh] = peak * scale + jnp.log(total)
            sv[group, 2 + hh] = jnp.sum(p * dp, axis=0, keepdims=True) * inverse

        loop(0, 2 * (xn + 1 - x), body)

        def to_rows(group):
            mask = owner_mask[...]
            parts = split3(jnp.concatenate([sv[group, k] * mask for k in range(4)], axis=0))
            flat = dot(parts, spread[...], 1, 1)
            flat = flat[: 4 * zn] + flat[4 * zn : 8 * zn] + flat[8 * zn :]
            out = flat[:zn]
            for k in range(1, 4):
                out = out + pltpu.roll(flat[k * zn : (k + 1) * zn], QB * k, 1)
            for i in range(zn):
                su[stage, group, i] = out[i : i + 1]

        loop(x, xn + 1, to_rows)

    def combine(stage):
        lane = lax.broadcasted_iota(jnp.int32, (1, HD), 1)

        def gather(i):
            aj[0, pl.ds(i, 1)] = su[stage, xn, i]
            for j in range(TOPK):
                c = sel[i, j]
                row = sr[stage][lax.div(c, zn), lax.rem(c, zn)]
                aj[1 + j, pl.ds(i, 1)] = jnp.where(c == seq, NEGATIVE, row)

        loop(0, zn, gather)
        every = [aj[j] for j in range(TOPK + 1)]
        peak = functools.reduce(jnp.maximum, every)
        total = functools.reduce(jnp.add, [jnp.exp(a - peak) for a in every])
        lse = peak + jnp.log(total)
        weights = [jnp.exp(a - lse) for a in every]
        delta = functools.reduce(
            jnp.add, [pltpu.roll(w, 2 * QB, 1) * a for w, a in zip(weights, every)]
        )
        own = jnp.where(lane < 2 * QB, weights[0], delta)
        for i in range(zn):
            wr[stage, xn, i] = own[i : i + 1]
            lr[i] = lse[i : i + 1]
            dr[i] = delta[i : i + 1]

        def slots(xd):
            for zd in range(zn):
                c = xd * zn + zd
                i = inv[c]
                line = jnp.where(flag[c] > 0, lr[i], -NEGATIVE)
                w = jnp.exp(sr[stage][xd, zd] - line)
                ws[stage, xd, zd] = jnp.where(lane < 2 * QB, w, dr[i])

        loop(0, xn, slots)

    def exchange(stage):
        flow = flow_stat[stage]
        up_first(su.at[stage], srx.at[stage], True, flow + 2)
        up_second(srx.at[stage], sr[stage], True, flow + 2)
        up_done(srx.at[stage], sr[stage], True, flow + 2)
        combine(stage)
        down_first(ws.at[stage], wrz.at[stage], True, flow)
        down_second(wrz.at[stage], wr.at[stage], True, flow)
        down_done(wrz.at[stage], wr.at[stage], True, flow)

    def gradients(stage):
        def to_lanes(group):
            m = jnp.concatenate([wr[stage, group, i] for i in range(zn)], axis=0)
            wide = [m] + [pltpu.roll(m, HD - QB * k, 1) for k in range(1, 4)]
            flat = dot(split3(jnp.concatenate(wide, axis=0)), spread[...], 1, 0)
            flat = flat[: 4 * zn] + flat[4 * zn : 8 * zn] + flat[8 * zn :]
            mask = owner_mask[...]
            for k in range(4):
                wv[group, k] = jnp.sum(flat[k * zn : (k + 1) * zn] * mask, axis=0, keepdims=True)

        loop(x, xn + 1, to_lanes)

        def body(step):
            hh = lax.rem(step, 2)
            group = x + lax.div(step, 2)
            h = 2 * stage + hh
            p = pb[hh, group] * (wv[group, hh] * li[hh, group])
            pr = p.astype(BF)
            ds = (p * (db[hh, group] - wv[group, 2 + hh])).astype(BF)
            out = dot(vt[h], pr, 1, 0).T.reshape(zn, QB, HD)
            dq = (dot(kt[h], ds, 1, 0) * scale).T.reshape(zn, QB, HD)
            rt[h, group] = jnp.concatenate([out, dq], axis=1).astype(BF)
            dk[h] += dot(ds, qc[hh, group], 1, 0)
            dv[h] += dot(pr, gc[hh, group], 1, 0)

        loop(0, 2 * (xn + 1 - x), body)

    def finish(stage):
        for h in (2 * stage, 2 * stage + 1):

            def body(i, h=h):
                acc = rt[h, xn, i].astype(F32)
                for j in range(TOPK):
                    c = sel[i, j]
                    part = gg[h][lax.div(c, zn), lax.rem(c, zn)].astype(F32)
                    acc = acc + jnp.where(c == seq, 0.0, part)
                fo[i] = acc

            loop(0, zn, body)
            cols = slice(h * HD, (h + 1) * HD)
            att[:, cols] = fo[:, :QB].reshape(tokens, HD).astype(BF)
            gq[:, cols] = fo[:, QB:].reshape(tokens, HD).astype(BF)
            gk[:, cols] = (dk[h] * scale).astype(BF)
            gv[:, cols] = dv[h].astype(BF)

    pack(0)
    forward_relay(1)
    pack(1)
    arrive(2)
    arrive(3)
    for h in range(heads):
        cols = slice(h * HD, (h + 1) * HD)
        kh[h] = ka[:, cols]
        vh[h] = va[:, cols]
        kt[h] = ka[:, cols].T
        vt[h] = va[:, cols].T
    dk[...] = jnp.zeros_like(dk)
    dv[...] = jnp.zeros_like(dv)
    forward_relay(3)
    forward_relay(0)
    down_done(r1.at[0], f.at[0], zfirst[0], flow_down[0])
    down_done(r1.at[1], f.at[1], zfirst[1], flow_down[1])
    scores(0)
    exchange(0)
    gradients(0)
    up_first(rt.at[0], r2.at[0], zfirst[0], flow_up[0])
    up_first(rt.at[1], r2.at[1], zfirst[1], flow_up[1])
    forward_relay(2)
    up_second(r2.at[0], gg[0], zfirst[0], flow_up[0])
    down_done(r1.at[2], f.at[2], zfirst[2], flow_down[2])
    down_done(r1.at[3], f.at[3], zfirst[3], flow_down[3])
    scores(1)
    exchange(1)
    gradients(1)
    up_first(rt.at[2], r2.at[2], zfirst[2], flow_up[2])
    up_first(rt.at[3], r2.at[3], zfirst[3], flow_up[3])
    up_second(r2.at[1], gg[1], zfirst[1], flow_up[1])
    up_second(r2.at[2], gg[2], zfirst[2], flow_up[2])
    up_done(r2.at[0], gg[0], zfirst[0], flow_up[0])
    up_done(r2.at[1], gg[1], zfirst[1], flow_up[1])
    finish(0)
    up_second(r2.at[3], gg[3], zfirst[3], flow_up[3])
    up_done(r2.at[2], gg[2], zfirst[2], flow_up[2])
    up_done(r2.at[3], gg[3], zfirst[3], flow_up[3])
    finish(1)

    for h in range(heads):
        drain(pk.at[h], zfirst[h], flow_down[h], True)
        drain(pk.at[h], zfirst[h], flow_up[h], False)
    for stage in range(heads // 2):
        drain(ws.at[stage], True, flow_stat[stage], True)
        drain(ws.at[stage], True, flow_stat[stage] + 2, False)
    for n, (src, dst) in enumerate(inputs):
        head_wait(dst, ssem.at[flow_head + n])


def local(mesh_seq, mesh_head, queries, keys, values, dout, selected):
    zn, hn = ZN, mesh_head
    xn = mesh_seq // zn
    rows, features = queries.shape
    heads = features // hn // HD
    tokens = rows * hn
    blocks = tokens // QB
    far = zn * QB
    width = heads * HD
    own = lax.axis_index("seq")
    slot = jnp.arange(mesh_seq, dtype=jnp.int32)
    hit = (selected[None] == slot[:, None, None]) & (selected[None] != own)
    hit = jnp.any(hit, axis=2)
    inv = jnp.sum(jnp.where(hit, jnp.arange(blocks, dtype=jnp.int32)[None], 0), axis=1)
    flag = jnp.sum(hit.astype(jnp.int32), axis=1)
    lane = np.arange(far)
    spread = jnp.asarray((np.arange(HD)[:, None] == lane[None] % QB).astype(np.float32), BF)
    owner_mask = jnp.asarray((np.arange(zn)[:, None] == lane[None] // QB).astype(np.float32))
    flows = 4 * heads + 4 * (heads // 2) + 4
    block = lambda groups: pltpu.VMEM((heads, groups, zn, 2 * QB, HD), BF)
    stat = lambda groups: pltpu.VMEM((heads // 2, groups, zn, 1, HD), F32)
    shape = jax.ShapeDtypeStruct((tokens, width), BF)
    smem = pl.BlockSpec(memory_space=pltpu.SMEM)
    vmem = pl.BlockSpec(memory_space=pltpu.VMEM)
    hbm = pl.BlockSpec(memory_space=pl.ANY)
    scratch = (
        [pltpu.VMEM((tokens, width), BF)] * 4
        + [pltpu.VMEM((blocks, QB, width), F32)] * 2
        + [pltpu.VMEM((heads, tokens, HD), BF)] * 2
        + [pltpu.VMEM((heads, HD, tokens), BF)] * 2
        + [block(xn), block(xn), block(xn + 1), block(xn + 1), block(xn)]
        + [pltpu.VMEM((xn, zn, 2 * QB, HD), BF)] * heads
        + [stat(xn + 1), stat(xn)]
        + [pltpu.VMEM((xn, zn, 1, HD), F32)] * (heads // 2)
        + [stat(xn), stat(xn), stat(xn + 1)]
        + [pltpu.VMEM((2, xn + 1, far, HD), BF)] * 2
        + [pltpu.VMEM((2, xn + 1, tokens, far), F32)] * 2
        + [pltpu.VMEM((2, xn + 1, 1, far), F32)]
        + [pltpu.VMEM((xn + 1, 4, 1, far), F32)] * 2
        + [pltpu.VMEM((heads, tokens, HD), F32)] * 2
        + [pltpu.VMEM((TOPK + 1, zn, HD), F32)]
        + [pltpu.VMEM((zn, 1, HD), F32)] * 2
        + [pltpu.VMEM((zn, 2 * QB, HD), F32)]
        + [pltpu.SemaphoreType.DMA((flows, zn))] * 2
        + [pltpu.SemaphoreType.DMA((4,))]
    )
    return pl.pallas_call(
        functools.partial(kernel, xn, zn, hn, heads),
        out_shape=(shape,) * 4,
        in_specs=[smem] * 3 + [vmem] * 2 + [hbm] * 4,
        out_specs=(vmem,) * 4,
        scratch_shapes=scratch,
        compiler_params=pltpu.CompilerParams(
            collective_id=0, has_side_effects=True, vmem_limit_bytes=VMEM_LIMIT
        ),
    )(selected, inv, flag, spread, owner_mask, queries, keys, values, dout)


def solution(mesh):
    tokens = P(("seq", "head"), None)
    out = P("seq", "head")
    return jax.shard_map(
        functools.partial(local, mesh.shape["seq"], mesh.shape["head"]),
        mesh=mesh,
        in_specs=(tokens,) * 4 + (P("seq", None),),
        out_specs=(out,) * 4,
        check_vma=False,
    )
```

time: 533 us -> 273 us (0.51)
  the two profiles are of different devices: /device:TPU:14 before, /device:TPU:30 now
where the time goes in v1:
time: 273 us; the launch traced here: 272 us
  Pallas kernels  265 us (97%)
  local copies, waits for them, and re-layouts  6.19 us (2%)
    pallas_call x1, Pallas kernels, local(): pl.pallas_call(functools.partial(kernel, xn, zn, hn, heads), out_shape=(s...  265 us
    unnamed x13, local copies, waits for them, and re-layouts  6.19 us

profile of v1, /device:TPU:30, one launch (start us, length us, event | category | flops | bytes accessed | tf_op | source)
XLA Modules:
  0.0 272.4 jit_solution(3891035776759398434)
XLA Ops:
  0.6 0.0 copy-start.3
  0.6 0.7 copy-done.3
  1.3 0.1 fusion.1
  1.4 0.5 convert_reduce_fusion
  1.9 0.7 copy.14.sel
  2.6 264.9 %shard_map.102 = (bf16[384,512]{1,0:T(8,128)(2,1)}, bf16[384,512]{1,0:T(8,128)(2,1)}, bf16[384,512]{1,0:T(8,128)(2,1)}, bf16[384,512]{1,0:T(8,128)(2,1)}) custom-call(s32[16,3]{1,0:T(8,128)} %copy.14.sel, s32[64]{0:T(128)} %get-tuple-element.5.inv, s32[64]{0:T(128)} %get-tuple-element.4.flag, bf16[128,384]{1,0:T(8,128)(2,1)} %constant.14.clone.spread, ...), custom_call_target="tpu_custom_call" | custom-call | tf_op jit(solution)/shard_map/pallas_call | solution.py:496
  267.5 0.0 copy-start.2
  267.5 1.8 copy.19
  269.4 0.0 copy-done.2
  269.4 0.0 copy-start.1
  269.4 0.7 copy.20
  270.1 0.4 copy-done.1
  270.5 0.0 copy-start
  270.5 0.7 copy.21
  271.3 0.4 copy-done
  271.6 0.7 copy.22
  (1 shorter events, 0.0 us)
Async XLA Ops:
  0.6 0.7 copy-start.3
  267.5 1.8 copy-start.2
  269.4 1.1 copy-start.1
  270.5 1.1 copy-start

commit v2 on v1

v2 whole, which is shorter than its diff:
```python
import functools
import math

import jax
import jax.numpy as jnp
import numpy as np
from jax import lax
from jax.experimental import pallas as pl
from jax.experimental.pallas import tpu as pltpu
from jax.sharding import PartitionSpec as P

HD = 128
QB = 24
TOPK = 3
ZN = 16
NEGATIVE = -1e30
MESH = pl.DeviceIdType.MESH
BF = jnp.bfloat16
F32 = jnp.float32
VMEM_LIMIT = 60 * 1024 * 1024


def dot(a, b, ca, cb):
    return lax.dot_general(a, b, (((ca,), (cb,)), ((), ())), preferred_element_type=F32)


def split3(a):
    high = a.astype(BF)
    rest = a - high.astype(F32)
    mid = rest.astype(BF)
    low = (rest - mid.astype(F32)).astype(BF)
    return jnp.concatenate([high, mid, low], axis=0)


def loop(start, stop, body):
    def step(index, carry):
        body(index)
        return carry

    lax.fori_loop(start, stop, step, 0)


def kernel(
    xn, zn, hn, heads,
    sel, inv, flag, spread, owner_mask, q_in, k_in, v_in, g_in,
    att, gq, gk, gv,
    qa, ka, va, ga, qf, gf, kh, vh, kt, vt,
    pk, r1, f, rt, r2, gg, su, srx, sr, ws, wrz, wr,
    qc, gc, pb, db, li, sv, wv, dk, dv, aj, lr, dr, fo,
    ssem, rsem, lsem,
):
    scale = 1.0 / math.sqrt(HD)
    seq = lax.axis_index("seq")
    head = lax.axis_index("head")
    x = lax.div(seq, zn)
    z = lax.rem(seq, zn)
    rows = q_in.shape[0]
    width = heads * HD
    tokens = qa.shape[0]
    far = zn * QB

    def z_partner(k):
        half = lax.div(k + 1, 2)
        return lax.rem(z + jnp.where(lax.rem(k, 2) == 1, half, zn - half), zn)

    def when(value, most, body):
        for m in range(1, most + 1):
            pl.when(value == m)(functools.partial(body, m))

    def wait(part, sem):
        pltpu.make_async_copy(part, part, sem).wait()

    def z_send(src, dst, lower, flow):
        start = 0 if lower else x + 1

        def send(m):
            def body(k):
                zi = z_partner(k)
                pltpu.make_async_remote_copy(
                    src_ref=src.at[pl.ds(start, m), zi],
                    dst_ref=dst.at[pl.ds(start, m), z],
                    send_sem=ssem.at[flow],
                    recv_sem=rsem.at[flow],
                    device_id={"seq": x * zn + zi},
                    device_id_type=MESH,
                ).start()

            loop(1, zn, body)

        when(x if lower else xn - 1 - x, xn - 1, send)

    def z_wait(buf, lower, sem):
        full = lambda m: wait(buf.at[pl.ds(0, m), pl.ds(0, zn - 1)], sem)
        when(x if lower else xn - 1 - x, xn - 1, full)

    def x_send(src, dst, down, flow):
        def body(xi):
            pltpu.make_async_remote_copy(
                src_ref=src.at[xi],
                dst_ref=dst.at[x],
                send_sem=ssem.at[flow],
                recv_sem=rsem.at[flow],
                device_id={"seq": xi * zn + z},
                device_id_type=MESH,
            ).start()

        if down:
            loop(0, x, body)
        else:
            loop(x + 1, xn, body)

    def x_wait(buf, down, sem, sent):
        full = lambda m: wait(buf.at[pl.ds(0, m)], sem)
        when(x if down == sent else xn - 1 - x, xn - 1, full)

    def near_send(src, dst, down, flow):
        def body(zi):
            pltpu.make_async_remote_copy(
                src_ref=src(zi),
                dst_ref=dst(z),
                send_sem=ssem.at[flow],
                recv_sem=rsem.at[flow],
                device_id={"seq": x * zn + zi},
                device_id_type=MESH,
            ).start()

        if down:
            loop(0, z, body)
        else:
            loop(z + 1, zn, body)

    def near_wait(part, down, sem, sent):
        when(z if down == sent else zn - 1 - z, zn - 1, lambda m: wait(part(m), sem))

    def bulk_at(ref):
        return lambda zi: ref.at[:, x, zi]

    def stat_at(ref):
        return lambda zi: ref.at[x, zi]

    def bulk_part(m):
        return pk.at[:, 0, pl.ds(0, m)]

    def stat_part(m):
        return ws.at[0, pl.ds(0, m)]

    def keep(dst, src, index):
        dst[index] = src[index]

    def down_first(src, mid, zf, flow):
        if zf:
            loop(0, x, lambda i: keep(mid, src, (i, z)))
            z_send(src, mid, True, flow)
        else:
            x_send(src, mid, True, flow)

    def down_second(mid, dst, zf, flow):
        if zf:
            z_wait(mid, True, rsem.at[flow])
            x_send(mid, dst, True, flow + 1)
        else:
            x_wait(mid, True, rsem.at[flow], False)
            z_send(mid, dst, False, flow + 1)

    def down_done(mid, dst, zf, flow):
        if zf:
            x_wait(dst, True, rsem.at[flow + 1], False)
        else:
            loop(x + 1, xn, lambda i: keep(dst, mid, (i, z)))
            z_wait(dst, False, rsem.at[flow + 1])

    def up_first(src, mid, zf, flow):
        if zf:
            x_send(src, mid, False, flow)
        else:
            loop(x + 1, xn, lambda i: keep(mid, src, (i, z)))
            z_send(src, mid, False, flow)

    def up_second(mid, dst, zf, flow):
        if zf:
            x_wait(mid, False, rsem.at[flow], False)
            z_send(mid, dst, True, flow + 1)
        else:
            z_wait(mid, False, rsem.at[flow])
            x_send(mid, dst, False, flow + 1)

    def up_done(mid, dst, zf, flow):
        if zf:
            loop(0, x, lambda i: keep(dst, mid, (i, z)))
            z_wait(dst, True, rsem.at[flow + 1])
        else:
            x_wait(dst, False, rsem.at[flow + 1], False)

    def drain(buf, zf, flow, down):
        first_z = zf if down else not zf
        z_flow = flow if first_z else flow + 1
        x_flow = flow + 1 if first_z else flow
        z_wait(buf, zf, ssem.at[z_flow])
        x_wait(buf, down, ssem.at[x_flow], True)

    zfirst = [h % 2 == 0 for h in range(heads)]
    flow_down = [4 * h for h in range(heads)]
    flow_up = [4 * h + 2 for h in range(heads)]
    flow_stat = 4 * heads
    flow_head = 4 * heads + 4
    flow_near = 4 * heads + 8

    def drain_heads():
        for n in range(4):
            head_wait(inputs[n][1], ssem.at[flow_head + n])

    f[...] = jnp.zeros_like(f)
    wr[...] = jnp.zeros_like(wr)
    sr[...] = jnp.zeros_like(sr)

    barrier = pltpu.get_barrier_semaphore()

    def greet(target):
        pl.semaphore_signal(barrier, inc=1, device_id=target, device_id_type=MESH)

    loop(1, hn, lambda i: greet({"head": lax.rem(head + i, hn)}))
    loop(1, zn, lambda i: greet({"seq": x * zn + lax.rem(z + i, zn)}))
    loop(1, xn, lambda i: greet({"seq": lax.rem(x + i, xn) * zn + z}))
    pl.semaphore_wait(barrier, hn + zn + xn - 3)

    inputs = ((q_in, qa), (g_in, ga), (k_in, ka), (v_in, va))
    here = pl.ds(pl.multiple_of(head * rows, rows), rows)

    def spread_heads(n):
        src, dst = inputs[n]

        def fan(i):
            hi = lax.rem(head + i, hn)
            pltpu.make_async_remote_copy(
                src_ref=src.at[:, pl.ds(pl.multiple_of(hi * width, width), width)],
                dst_ref=dst.at[here],
                send_sem=ssem.at[flow_head + n],
                recv_sem=rsem.at[flow_head + n],
                device_id={"head": hi},
                device_id_type=MESH,
            ).start()

        loop(1, hn, fan)
        pltpu.make_async_copy(
            src.at[:, pl.ds(pl.multiple_of(head * width, width), width)], dst.at[here], lsem.at[n]
        ).start()

    def head_wait(dst, sem):
        if hn > 1:
            wait(dst.at[pl.ds(0, (hn - 1) * rows)], sem)

    def arrive(n):
        src, dst = inputs[n]
        pltpu.make_async_copy(
            src.at[:, pl.ds(pl.multiple_of(head * width, width), width)], dst.at[here], lsem.at[n]
        ).wait()
        head_wait(dst, rsem.at[flow_head + n])

    spread_heads(0)
    spread_heads(1)
    arrive(0)
    qf[...] = qa[...].astype(F32).reshape(qf.shape)
    arrive(1)
    gf[...] = ga[...].astype(F32).reshape(gf.shape)
    spread_heads(2)
    spread_heads(3)

    def block_of(i, h):
        cols = slice(h * HD, (h + 1) * HD)
        return jnp.concatenate([qf[i, :, cols], gf[i, :, cols]], axis=0).astype(BF)

    def pack(stage):
        def body(zd):
            for h in (2 * stage, 2 * stage + 1):
                f[h, xn, zd] = block_of(zd, h)
            for xd in range(xn):
                i = inv[xd * zn + zd]
                for h in (2 * stage, 2 * stage + 1):
                    pk[h, xd, zd] = block_of(i, h)

        loop(0, zn, body)

    def start_down(h):
        down_first(pk.at[h], r1.at[h], zfirst[h], flow_down[h])

    def forward_relay(h):
        down_second(r1.at[h], f.at[h], zfirst[h], flow_down[h])

    def arrived(h):
        down_done(r1.at[h], f.at[h], zfirst[h], flow_down[h])

    def start_up(h):
        up_first(rt.at[h], r2.at[h], zfirst[h], flow_up[h])

    def return_relay(h):
        up_second(r2.at[h], gg.at[h], zfirst[h], flow_up[h])

    def returned(h):
        up_done(r2.at[h], gg.at[h], zfirst[h], flow_up[h])

    def scores(h, first, last):
        u = lax.broadcasted_iota(jnp.int32, (tokens, far), 0)
        t = lax.broadcasted_iota(jnp.int32, (tokens, far), 1)

        def body(group):
            both = f[h, group].astype(F32)
            qv = both[:, :QB].reshape(far, HD).astype(BF)
            gv_ = both[:, QB:].reshape(far, HD).astype(BF)
            qc[h, group] = qv
            gc[h, group] = gv_
            s = dot(kh[h], qv, 1, 1)
            dp = dot(vh[h], gv_, 1, 1)
            s = jnp.where(u <= t + jnp.where(group == xn, 0, tokens), s, NEGATIVE)
            peak = jnp.max(s, axis=0, keepdims=True)
            p = jnp.exp((s - peak) * scale)
            total = jnp.sum(p, axis=0, keepdims=True)
            pb[h, group] = p
            db[h, group] = dp
            inverse = 1.0 / total
            li[h, group] = inverse
            sv[group, h] = peak * scale + jnp.log(total)
            sv[group, heads + h] = jnp.sum(p * dp, axis=0, keepdims=True) * inverse

        loop(first, last, body)

    def statistics(stage):
        picks = (2 * stage, 2 * stage + 1, heads + 2 * stage, heads + 2 * stage + 1)

        def to_rows(group):
            mask = owner_mask[...]
            parts = split3(jnp.concatenate([sv[group, k] * mask for k in picks], axis=0))
            flat = dot(parts, spread[...], 1, 1)
            flat = flat[: 4 * zn] + flat[4 * zn : 8 * zn] + flat[8 * zn :]
            out = flat[:zn]
            for k in range(1, 4):
                out = out + pltpu.roll(flat[k * zn : (k + 1) * zn], QB * k, 1)
            for i in range(zn):
                su[group, i, pl.ds(stage, 1)] = out[i : i + 1]

        loop(x, xn + 1, to_rows)

    def combine(stage):
        lane = lax.broadcasted_iota(jnp.int32, (1, HD), 1)

        def gather(i):
            aj[0, pl.ds(i, 1)] = su[xn, i, pl.ds(stage, 1)]
            for j in range(TOPK):
                c = sel[i, j]
                row = sr[lax.div(c, zn), lax.rem(c, zn), pl.ds(stage, 1)]
                aj[1 + j, pl.ds(i, 1)] = jnp.where(c == seq, NEGATIVE, row)

        loop(0, zn, gather)
        every = [aj[j] for j in range(TOPK + 1)]
        peak = functools.reduce(jnp.maximum, every)
        total = functools.reduce(jnp.add, [jnp.exp(a - peak) for a in every])
        lse = peak + jnp.log(total)
        weights = [jnp.exp(a - lse) for a in every]
        delta = functools.reduce(
            jnp.add, [pltpu.roll(w, 2 * QB, 1) * a for w, a in zip(weights, every)]
        )
        own = jnp.where(lane < 2 * QB, weights[0], delta)
        for i in range(zn):
            wr[xn, i, pl.ds(stage, 1)] = own[i : i + 1]
            lr[i] = lse[i : i + 1]
            dr[i] = delta[i : i + 1]

        def slots(xd):
            for zd in range(zn):
                c = xd * zn + zd
                i = inv[c]
                line = jnp.where(flag[c] > 0, lr[i], -NEGATIVE)
                w = jnp.exp(sr[xd, zd, pl.ds(stage, 1)] - line)
                ws[xd, zd, pl.ds(stage, 1)] = jnp.where(lane < 2 * QB, w, dr[i])

        loop(0, xn, slots)

    def weights_of(stage):
        def to_lanes(group):
            m = jnp.concatenate([wr[group, i, pl.ds(stage, 1)] for i in range(zn)], axis=0)
            wide = [m] + [pltpu.roll(m, HD - QB * k, 1) for k in range(1, 4)]
            flat = dot(split3(jnp.concatenate(wide, axis=0)), spread[...], 1, 0)
            flat = flat[: 4 * zn] + flat[4 * zn : 8 * zn] + flat[8 * zn :]
            mask = owner_mask[...]
            for k, pick in enumerate((2 * stage, 2 * stage + 1, heads + 2 * stage, heads + 2 * stage + 1)):
                wv[group, pick] = jnp.sum(flat[k * zn : (k + 1) * zn] * mask, axis=0, keepdims=True)

        loop(x, xn + 1, to_lanes)

    def gradients(h, first, last):
        def body(group):
            p = pb[h, group] * (wv[group, h] * li[h, group])
            pr = p.astype(BF)
            ds = (p * (db[h, group] - wv[group, heads + h])).astype(BF)
            out = dot(vt[h], pr, 1, 0).T.reshape(zn, QB, HD)
            dq = (dot(kt[h], ds, 1, 0) * scale).T.reshape(zn, QB, HD)
            rt[h, group] = jnp.concatenate([out, dq], axis=1).astype(BF)
            dk[h] += dot(ds, qc[h, group], 1, 0)
            dv[h] += dot(pr, gc[h, group], 1, 0)

        loop(first, last, body)

    def finish(h):
        def body(i):
            acc = rt[h, xn, i].astype(F32)
            for j in range(TOPK):
                c = sel[i, j]
                part = gg[h, lax.div(c, zn), lax.rem(c, zn)].astype(F32)
                acc = acc + jnp.where(c == seq, 0.0, part)
            fo[i] = acc

        loop(0, zn, body)
        cols = slice(h * HD, (h + 1) * HD)
        att[:, cols] = fo[:, :QB].reshape(tokens, HD).astype(BF)
        gq[:, cols] = fo[:, QB:].reshape(tokens, HD).astype(BF)

    def finish_keys(h):
        cols = slice(h * HD, (h + 1) * HD)
        gk[:, cols] = (dk[h] * scale).astype(BF)
        gv[:, cols] = dv[h].astype(BF)

    def key_heads():
        for h in range(heads):
            cols = slice(h * HD, (h + 1) * HD)
            kh[h] = ka[:, cols]
            vh[h] = va[:, cols]
            kt[h] = ka[:, cols].T
            vt[h] = va[:, cols].T
        dk[...] = jnp.zeros_like(dk)
        dv[...] = jnp.zeros_like(dv)

    near = flow_near
    pack(0)
    pack(1)
    start_down(1)
    start_down(3)
    pl.when(x < xn // 2)(lambda: near_send(bulk_at(pk), bulk_at(f), True, near))
    start_down(0)
    start_down(2)
    pl.when(x >= xn // 2)(lambda: near_send(bulk_at(pk), bulk_at(f), True, near))
    forward_relay(1)
    arrive(2)
    arrive(3)
    key_heads()
    forward_relay(3)
    forward_relay(0)
    arrived(0)
    scores(0, x + 1, xn + 1)
    arrived(1)
    scores(1, x + 1, xn + 1)
    forward_relay(2)
    near_wait(bulk_part, True, rsem.at[near], False)
    loop(0, heads, lambda h: scores(h, x, x + 1))
    statistics(0)
    arrived(2)
    scores(2, x + 1, xn + 1)
    arrived(3)
    scores(3, x + 1, xn + 1)
    statistics(1)
    up_first(su, srx, True, flow_stat + 2)
    near_send(stat_at(su), stat_at(sr), False, near + 3)
    up_second(srx, sr, True, flow_stat + 2)
    up_done(srx, sr, True, flow_stat + 2)
    near_wait(stat_part, False, rsem.at[near + 3], False)
    combine(0)
    combine(1)
    down_first(ws, wrz, True, flow_stat)
    near_send(stat_at(ws), stat_at(wr), True, near + 2)
    down_second(wrz, wr, True, flow_stat)
    down_done(wrz, wr, True, flow_stat)
    near_wait(stat_part, True, rsem.at[near + 2], False)
    weights_of(0)
    gradients(0, x + 1, xn + 1)
    start_up(0)
    gradients(1, x + 1, xn + 1)
    start_up(1)
    weights_of(1)
    loop(0, heads, lambda h: gradients(h, x, x + 1))
    pl.when(x >= xn // 2)(lambda: near_send(bulk_at(rt), bulk_at(gg), False, near + 1))
    gradients(2, x + 1, xn + 1)
    start_up(2)
    return_relay(0)
    gradients(3, x + 1, xn + 1)
    start_up(3)
    pl.when(x < xn // 2)(lambda: near_send(bulk_at(rt), bulk_at(gg), False, near + 1))
    return_relay(2)
    finish_keys(0)
    finish_keys(1)
    finish_keys(2)
    finish_keys(3)
    return_relay(1)
    return_relay(3)
    drain_heads()
    for h in range(heads):
        drain(pk.at[h], zfirst[h], flow_down[h], True)
    drain(ws, True, flow_stat, True)
    drain(ws, True, flow_stat + 2, False)
    near_wait(bulk_part, True, ssem.at[near], True)
    near_wait(stat_part, True, ssem.at[near + 2], True)
    near_wait(stat_part, False, ssem.at[near + 3], True)
    returned(0)
    returned(1)
    returned(2)
    returned(3)
    near_wait(bulk_part, False, rsem.at[near + 1], False)
    finish(0)
    finish(1)
    finish(2)
    finish(3)
    for h in range(heads):
        drain(pk.at[h], zfirst[h], flow_up[h], False)
    near_wait(bulk_part, False, ssem.at[near + 1], True)


def local(mesh_seq, mesh_head, queries, keys, values, dout, selected):
    zn, hn = ZN, mesh_head
    xn = mesh_seq // zn
    rows, features = queries.shape
    heads = features // hn // HD
    tokens = rows * hn
    blocks = tokens // QB
    far = zn * QB
    width = heads * HD
    own = lax.axis_index("seq")
    slot = jnp.arange(mesh_seq, dtype=jnp.int32)
    hit = (selected[None] == slot[:, None, None]) & (selected[None] != own)
    hit = jnp.any(hit, axis=2)
    inv = jnp.sum(jnp.where(hit, jnp.arange(blocks, dtype=jnp.int32)[None], 0), axis=1)
    flag = jnp.sum(hit.astype(jnp.int32), axis=1)
    lane = np.arange(far)
    spread = jnp.asarray((np.arange(HD)[:, None] == lane[None] % QB).astype(np.float32), BF)
    owner_mask = jnp.asarray((np.arange(zn)[:, None] == lane[None] // QB).astype(np.float32))
    flows = 4 * heads + 12
    block = lambda groups: pltpu.VMEM((heads, groups, zn, 2 * QB, HD), BF)
    stat = lambda groups: pltpu.VMEM((groups, zn, heads // 2, HD), F32)
    shape = jax.ShapeDtypeStruct((tokens, width), BF)
    smem = pl.BlockSpec(memory_space=pltpu.SMEM)
    vmem = pl.BlockSpec(memory_space=pltpu.VMEM)
    hbm = pl.BlockSpec(memory_space=pl.ANY)
    scratch = (
        [pltpu.VMEM((tokens, width), BF)] * 4
        + [pltpu.VMEM((blocks, QB, width), F32)] * 2
        + [pltpu.VMEM((heads, tokens, HD), BF)] * 2
        + [pltpu.VMEM((heads, HD, tokens), BF)] * 2
        + [block(xn), block(xn), block(xn + 1), block(xn + 1), block(xn), block(xn)]
        + [stat(xn + 1), stat(xn), stat(xn), stat(xn), stat(xn), stat(xn + 1)]
        + [pltpu.VMEM((heads, xn + 1, far, HD), BF)] * 2
        + [pltpu.VMEM((heads, xn + 1, tokens, far), F32)] * 2
        + [pltpu.VMEM((heads, xn + 1, 1, far), F32)]
        + [pltpu.VMEM((xn + 1, 2 * heads, 1, far), F32)] * 2
        + [pltpu.VMEM((heads, tokens, HD), F32)] * 2
        + [pltpu.VMEM((TOPK + 1, zn, HD), F32)]
        + [pltpu.VMEM((zn, 1, HD), F32)] * 2
        + [pltpu.VMEM((zn, 2 * QB, HD), F32)]
        + [pltpu.SemaphoreType.DMA((flows,))] * 2
        + [pltpu.SemaphoreType.DMA((4,))]
    )
    return pl.pallas_call(
        functools.partial(kernel, xn, zn, hn, heads),
        out_shape=(shape,) * 4,
        in_specs=[smem] * 3 + [vmem] * 2 + [hbm] * 4,
        out_specs=(vmem,) * 4,
        scratch_shapes=scratch,
        compiler_params=pltpu.CompilerParams(
            collective_id=0, has_side_effects=True, vmem_limit_bytes=VMEM_LIMIT
        ),
    )(selected, inv, flag, spread, owner_mask, queries, keys, values, dout)


def solution(mesh):
    tokens = P(("seq", "head"), None)
    out = P("seq", "head")
    return jax.shard_map(
        functools.partial(local, mesh.shape["seq"], mesh.shape["head"]),
        mesh=mesh,
        in_specs=(tokens,) * 4 + (P("seq", None),),
        out_specs=(out,) * 4,
        check_vma=False,
    )
```

time: 273 us -> 247 us (0.905)
  the two profiles are of different devices: /device:TPU:30 before, /device:TPU:456 now
where the time goes in v2:
time: 247 us; the launch traced here: 246 us
  Pallas kernels  239 us (97%)
  local copies, waits for them, and re-layouts  6.19 us (3%)
    pallas_call x1, Pallas kernels, local(): pl.pallas_call(functools.partial(kernel, xn, zn, hn, heads), out_shape=(s...  239 us
    unnamed x13, local copies, waits for them, and re-layouts  6.19 us

profile of v2, /device:TPU:456, one launch (start us, length us, event | category | flops | bytes accessed | tf_op | source)
XLA Modules:
  0.0 246.5 jit_solution(17916876352348804721)
XLA Ops:
  0.6 0.0 copy-start.3
  0.6 0.7 copy-done.3
  1.3 0.1 fusion.1
  1.4 0.5 convert_reduce_fusion
  1.9 0.7 copy.14.sel
  2.6 239.0 %shard_map.102 = (bf16[384,512]{1,0:T(8,128)(2,1)}, bf16[384,512]{1,0:T(8,128)(2,1)}, bf16[384,512]{1,0:T(8,128)(2,1)}, bf16[384,512]{1,0:T(8,128)(2,1)}) custom-call(s32[16,3]{1,0:T(8,128)} %copy.14.sel, s32[64]{0:T(128)} %get-tuple-element.5.inv, s32[64]{0:T(128)} %get-tuple-element.4.flag, bf16[128,384]{1,0:T(8,128)(2,1)} %constant.14.clone.spread, ...), custom_call_target="tpu_custom_call" | custom-call | tf_op jit(solution)/shard_map/pallas_call | solution.py:557
  241.6 0.0 copy-start.2
  241.6 1.8 copy.19
  243.5 0.0 copy-done.2
  243.5 0.0 copy-start.1
  243.5 0.7 copy.20
  244.2 0.4 copy-done.1
  244.6 0.0 copy-start
  244.6 0.7 copy.21
  245.3 0.4 copy-done
  245.7 0.7 copy.22
  (1 shorter events, 0.0 us)
Async XLA Ops:
  0.6 0.7 copy-start.3
  241.6 1.8 copy-start.2
  243.5 1.1 copy-start.1
  244.6 1.1 copy-start

commit v3 on v2

--- a/solution.py
+++ b/solution.py
@@ -45,8 +45,8 @@
     sel, inv, flag, spread, owner_mask, q_in, k_in, v_in, g_in,
     att, gq, gk, gv,
     qa, ka, va, ga, qf, gf, kh, vh, kt, vt,
-    pk, r1, f, rt, r2, gg, su, srx, sr, ws, wrz, wr,
-    qc, gc, pb, db, li, sv, wv, dk, dv, aj, lr, dr, fo,
+    pk, r1, f, rt, r2, go, gd, su, srx, sr, ws, wrz, wr,
+    qc, gc, pb, db, li, sv, wv, dk, dv, aj, lr, dr, fo, ob, wt,
     ssem, rsem, lsem,
 ):
     scale = 1.0 / math.sqrt(HD)
@@ -135,6 +135,12 @@
     def bulk_at(ref):
         return lambda zi: ref.at[:, x, zi]
 
+    def pair_at(ref, first):
+        return lambda zi: ref.at[pl.ds(first, heads // 2), x, zi]
+
+    def pair_part(m):
+        return pk.at[pl.ds(0, heads // 2), 0, pl.ds(0, m)]
+
     def stat_at(ref):
         return lambda zi: ref.at[x, zi]
 
@@ -203,11 +209,11 @@
     flow_up = [4 * h + 2 for h in range(heads)]
     flow_stat = 4 * heads
     flow_head = 4 * heads + 4
-    flow_near = 4 * heads + 8
+    flow_near = 4 * heads + 10
 
     def drain_heads():
-        for n in range(4):
-            head_wait(inputs[n][1], ssem.at[flow_head + n])
+        for n in range(6):
+            head_wait(n, ssem.at[flow_head + n])
 
     f[...] = jnp.zeros_like(f)
     wr[...] = jnp.zeros_like(wr)
@@ -223,17 +229,24 @@
     loop(1, xn, lambda i: greet({"seq": lax.rem(x + i, xn) * zn + z}))
     pl.semaphore_wait(barrier, hn + zn + xn - 3)
 
-    inputs = ((q_in, qa), (g_in, ga), (k_in, ka), (v_in, va))
+    half = width // 2
+    inputs = (
+        (q_in, qa, 0, half), (g_in, ga, 0, half), (q_in, qa, half, half), (g_in, ga, half, half),
+        (k_in, ka, 0, width), (v_in, va, 0, width),
+    )
     here = pl.ds(pl.multiple_of(head * rows, rows), rows)
 
+    def columns(device, first, count):
+        return pl.ds(pl.multiple_of(device * width + first, half), count)
+
     def spread_heads(n):
-        src, dst = inputs[n]
+        src, dst, first, count = inputs[n]
 
         def fan(i):
             hi = lax.rem(head + i, hn)
             pltpu.make_async_remote_copy(
-                src_ref=src.at[:, pl.ds(pl.multiple_of(hi * width, width), width)],
-                dst_ref=dst.at[here],
+                src_ref=src.at[:, columns(hi, first, count)],
+                dst_ref=dst.at[here, pl.ds(first, count)],
                 send_sem=ssem.at[flow_head + n],
                 recv_sem=rsem.at[flow_head + n],
                 device_id={"head": hi},
@@ -242,28 +255,33 @@
 
         loop(1, hn, fan)
         pltpu.make_async_copy(
-            src.at[:, pl.ds(pl.multiple_of(head * width, width), width)], dst.at[here], lsem.at[n]
+            src.at[:, columns(head, first, count)], dst.at[here, pl.ds(first, count)], lsem.at[n]
         ).start()
 
-    def head_wait(dst, sem):
+    def head_wait(n, sem):
+        src, dst, first, count = inputs[n]
         if hn > 1:
-            wait(dst.at[pl.ds(0, (hn - 1) * rows)], sem)
+            wait(dst.at[pl.ds(0, (hn - 1) * rows), pl.ds(first, count)], sem)
 
     def arrive(n):
-        src, dst = inputs[n]
+        src, dst, first, count = inputs[n]
         pltpu.make_async_copy(
-            src.at[:, pl.ds(pl.multiple_of(head * width, width), width)], dst.at[here], lsem.at[n]
+            src.at[:, columns(head, first, count)], dst.at[here, pl.ds(first, count)], lsem.at[n]
         ).wait()
-        head_wait(dst, rsem.at[flow_head + n])
-
-    spread_heads(0)
-    spread_heads(1)
-    arrive(0)
-    qf[...] = qa[...].astype(F32).reshape(qf.shape)
-    arrive(1)
-    gf[...] = ga[...].astype(F32).reshape(gf.shape)
-    spread_heads(2)
-    spread_heads(3)
+        head_wait(n, rsem.at[flow_head + n])
+
+    def widen(dst, src, first):
+        part = src[:, first : first + half].astype(F32)
+        dst[:, :, first : first + half] = part.reshape(tokens // QB, QB, half)
+
+    def arrive_half(k):
+        arrive(2 * k)
+        widen(qf, qa, k * half)
+        arrive(2 * k + 1)
+        widen(gf, ga, k * half)
+
+    for n in range(6):
+        spread_heads(n)
 
     def block_of(i, h):
         cols = slice(h * HD, (h + 1) * HD)
@@ -280,6 +298,8 @@
 
         loop(0, zn, body)
 
+    back = [go.at[0], go.at[1], gd.at[0], gd.at[1]]
+
     def start_down(h):
         down_first(pk.at[h], r1.at[h], zfirst[h], flow_down[h])
 
@@ -293,37 +313,53 @@
         up_first(rt.at[h], r2.at[h], zfirst[h], flow_up[h])
 
     def return_relay(h):
-        up_second(r2.at[h], gg.at[h], zfirst[h], flow_up[h])
+        up_second(r2.at[h], back[h], zfirst[h], flow_up[h])
 
     def returned(h):
-        up_done(r2.at[h], gg.at[h], zfirst[h], flow_up[h])
-
-    def scores(h, first, last):
+        up_done(r2.at[h], back[h], zfirst[h], flow_up[h])
+
+    def score_one(h, group):
         u = lax.broadcasted_iota(jnp.int32, (tokens, far), 0)
         t = lax.broadcasted_iota(jnp.int32, (tokens, far), 1)
-
+        both = f[h, group].astype(F32)
+        qv = both[:, :QB].reshape(far, HD).astype(BF)
+        gv_ = both[:, QB:].reshape(far, HD).astype(BF)
+        qc[h, group] = qv
+        gc[h, group] = gv_
+        s = dot(kh[h], qv, 1, 1)
+        dp = dot(vh[h], gv_, 1, 1)
+        s = jnp.where(u <= t + jnp.where(group == xn, 0, tokens), s, NEGATIVE)
+        peak = jnp.max(s, axis=0, keepdims=True)
+        p = jnp.exp((s - peak) * scale)
+        total = jnp.sum(p, axis=0, keepdims=True)
+        pb[h, group] = p
+        db[h, group] = dp
+        inverse = 1.0 / total
+        li[h, group] = inverse
+        sv[group, h] = peak * scale + jnp.log(total)
+        sv[group, heads + h] = jnp.sum(p * dp, axis=0, keepdims=True) * inverse
+        return (dot(vt[h], p.astype(BF), 1, 0) * inverse).T.reshape(zn, QB, HD)
+
+    def scores(h):
         def body(group):
-            both = f[h, group].astype(F32)
-            qv = both[:, :QB].reshape(far, HD).astype(BF)
-            gv_ = both[:, QB:].reshape(far, HD).astype(BF)
-            qc[h, group] = qv
-            gc[h, group] = gv_
-            s = dot(kh[h], qv, 1, 1)
-            dp = dot(vh[h], gv_, 1, 1)
-            s = jnp.where(u <= t + jnp.where(group == xn, 0, tokens), s, NEGATIVE)
-            peak = jnp.max(s, axis=0, keepdims=True)
-            p = jnp.exp((s - peak) * scale)
-            total = jnp.sum(p, axis=0, keepdims=True)
-            pb[h, group] = p
-            db[h, group] = dp
-            inverse = 1.0 / total
-            li[h, group] = inverse
-            sv[group, h] = peak * scale + jnp.log(total)
-            sv[group, heads + h] = jnp.sum(p * dp, axis=0, keepdims=True) * inverse
-
-        loop(first, last, body)
-
-    def statistics(stage):
+            out = score_one(h, group)
+            if h % 2 == 0:
+                ob[h // 2, group] = out
+            else:
+                rt[h // 2, group] = jnp.concatenate([ob[h // 2, group], out], axis=1).astype(BF)
+
+        loop(x + 1, xn + 1, body)
+
+    def near_scores():
+        near_wait(bulk_part, True, rsem.at[near], False)
+
+        def body(stage):
+            both = [score_one(2 * stage, x), score_one(2 * stage + 1, x)]
+            rt[stage, x] = jnp.concatenate(both, axis=1).astype(BF)
+
+        loop(0, heads // 2, body)
+
+    def statistics(stage, first, last):
         picks = (2 * stage, 2 * stage + 1, heads + 2 * stage, heads + 2 * stage + 1)
 
         def to_rows(group):
@@ -337,7 +373,7 @@
             for i in range(zn):
                 su[group, i, pl.ds(stage, 1)] = out[i : i + 1]
 
-        loop(x, xn + 1, to_rows)
+        loop(first, last, to_rows)
 
     def combine(stage):
         lane = lax.broadcasted_iota(jnp.int32, (1, HD), 1)
@@ -359,6 +395,8 @@
             jnp.add, [pltpu.roll(w, 2 * QB, 1) * a for w, a in zip(weights, every)]
         )
         own = jnp.where(lane < 2 * QB, weights[0], delta)
+        for j in range(TOPK + 1):
+            wt[stage, j] = weights[j].T
         for i in range(zn):
             wr[xn, i, pl.ds(stage, 1)] = own[i : i + 1]
             lr[i] = lse[i : i + 1]
@@ -386,32 +424,48 @@
 
         loop(x, xn + 1, to_lanes)
 
-    def gradients(h, first, last):
-        def body(group):
+    def gradients(stage):
+        def part(h, group):
             p = pb[h, group] * (wv[group, h] * li[h, group])
             pr = p.astype(BF)
             ds = (p * (db[h, group] - wv[group, heads + h])).astype(BF)
-            out = dot(vt[h], pr, 1, 0).T.reshape(zn, QB, HD)
-            dq = (dot(kt[h], ds, 1, 0) * scale).T.reshape(zn, QB, HD)
-            rt[h, group] = jnp.concatenate([out, dq], axis=1).astype(BF)
             dk[h] += dot(ds, qc[h, group], 1, 0)
             dv[h] += dot(pr, gc[h, group], 1, 0)
-
-        loop(first, last, body)
-
-    def finish(h):
-        def body(i):
-            acc = rt[h, xn, i].astype(F32)
+            return (dot(kt[h], ds, 1, 0) * scale).T.reshape(zn, QB, HD)
+
+        def body(group):
+            both = [part(2 * stage, group), part(2 * stage + 1, group)]
+            rt[heads // 2 + stage, group] = jnp.concatenate(both, axis=1).astype(BF)
+
+        loop(x, xn + 1, body)
+
+    def unpack(dst, stage):
+        for k in range(2):
+            h = 2 * stage + k
+            dst[:, h * HD : (h + 1) * HD] = fo[:, k * QB : (k + 1) * QB].reshape(tokens, HD).astype(BF)
+
+    def finish_attended(stage):
+        for i in range(zn):
+            acc = wt[stage, 0, : 2 * QB, i : i + 1] * rt[stage, xn, i].astype(F32)
             for j in range(TOPK):
                 c = sel[i, j]
-                part = gg[h, lax.div(c, zn), lax.rem(c, zn)].astype(F32)
+                part = go[stage, lax.div(c, zn), lax.rem(c, zn)].astype(F32)
+                part = wt[stage, 1 + j, : 2 * QB, i : i + 1] * part
                 acc = acc + jnp.where(c == seq, 0.0, part)
             fo[i] = acc
+        unpack(att, stage)
+
+    def finish_queries(stage):
+        def body(i):
+            acc = rt[heads // 2 + stage, xn, i].astype(F32)
+            for j in range(TOPK):
+                c = sel[i, j]
+                part = gd[stage, lax.div(c, zn), lax.rem(c, zn)].astype(F32)
+                acc = acc + jnp.where(c == seq, 0.0, part)
+            fo[i] = acc
 
         loop(0, zn, body)
-        cols = slice(h * HD, (h + 1) * HD)
-        att[:, cols] = fo[:, :QB].reshape(tokens, HD).astype(BF)
-        gq[:, cols] = fo[:, QB:].reshape(tokens, HD).astype(BF)
+        unpack(gq, stage)
 
     def finish_keys(h):
         cols = slice(h * HD, (h + 1) * HD)
@@ -429,86 +483,92 @@
         dv[...] = jnp.zeros_like(dv)
 
     near = flow_near
+    near_out, near_dq = near + 1, near + 4
+    arrive_half(0)
     pack(0)
+    start_down(1)
+    start_down(0)
+    arrive_half(1)
     pack(1)
-    start_down(1)
+    pl.when(x == 0)(lambda: near_send(bulk_at(pk), bulk_at(f), True, near))
+    start_down(2)
+    pl.when(x == xn - 1)(lambda: near_send(bulk_at(pk), bulk_at(f), True, near))
+    forward_relay(1)
+    x_wait(pk.at[1], True, ssem.at[flow_down[1]], True)
     start_down(3)
-    pl.when(x < xn // 2)(lambda: near_send(bulk_at(pk), bulk_at(f), True, near))
-    start_down(0)
-    start_down(2)
-    pl.when(x >= xn // 2)(lambda: near_send(bulk_at(pk), bulk_at(f), True, near))
-    forward_relay(1)
-    arrive(2)
-    arrive(3)
+    arrive(4)
+    arrive(5)
     key_heads()
+    forward_relay(0)
     forward_relay(3)
-    forward_relay(0)
+    pl.when((x > 0) & (x < xn - 1))(lambda: near_send(bulk_at(pk), bulk_at(f), True, near))
+    forward_relay(2)
     arrived(0)
-    scores(0, x + 1, xn + 1)
+    scores(0)
     arrived(1)
-    scores(1, x + 1, xn + 1)
-    forward_relay(2)
-    near_wait(bulk_part, True, rsem.at[near], False)
-    loop(0, heads, lambda h: scores(h, x, x + 1))
-    statistics(0)
+    scores(1)
+    statistics(0, x + 1, xn + 1)
+    pl.when(x == 0)(near_scores)
     arrived(2)
-    scores(2, x + 1, xn + 1)
+    scores(2)
     arrived(3)
-    scores(3, x + 1, xn + 1)
-    statistics(1)
+    scores(3)
+    statistics(1, x + 1, xn + 1)
+    pl.when(x > 0)(near_scores)
+    statistics(0, x, x + 1)
+    statistics(1, x, x + 1)
     up_first(su, srx, True, flow_stat + 2)
     near_send(stat_at(su), stat_at(sr), False, near + 3)
+    start_up(0)
     up_second(srx, sr, True, flow_stat + 2)
+    near_send(pair_at(rt, 0), lambda zi: go.at[:, x, zi], False, near_out)
     up_done(srx, sr, True, flow_stat + 2)
     near_wait(stat_part, False, rsem.at[near + 3], False)
     combine(0)
     combine(1)
     down_first(ws, wrz, True, flow_stat)
     near_send(stat_at(ws), stat_at(wr), True, near + 2)
+    start_up(1)
+    return_relay(0)
     down_second(wrz, wr, True, flow_stat)
     down_done(wrz, wr, True, flow_stat)
     near_wait(stat_part, True, rsem.at[near + 2], False)
     weights_of(0)
-    gradients(0, x + 1, xn + 1)
-    start_up(0)
-    gradients(1, x + 1, xn + 1)
-    start_up(1)
+    gradients(0)
+    start_up(2)
     weights_of(1)
-    loop(0, heads, lambda h: gradients(h, x, x + 1))
-    pl.when(x >= xn // 2)(lambda: near_send(bulk_at(rt), bulk_at(gg), False, near + 1))
-    gradients(2, x + 1, xn + 1)
-    start_up(2)
-    return_relay(0)
-    gradients(3, x + 1, xn + 1)
+    gradients(1)
     start_up(3)
-    pl.when(x < xn // 2)(lambda: near_send(bulk_at(rt), bulk_at(gg), False, near + 1))
+    near_send(pair_at(rt, 2), lambda zi: gd.at[:, x, zi], False, near_dq)
+    return_relay(1)
     return_relay(2)
-    finish_keys(0)
-    finish_keys(1)
-    finish_keys(2)
-    finish_keys(3)
-    return_relay(1)
+    for h in range(heads):
+        finish_keys(h)
+    returned(0)
+    returned(1)
+    near_wait(pair_part, False, rsem.at[near_out], False)
+    finish_attended(0)
+    finish_attended(1)
     return_relay(3)
     drain_heads()
     for h in range(heads):
-        drain(pk.at[h], zfirst[h], flow_down[h], True)
+        z_wait(pk.at[h], zfirst[h], ssem.at[flow_down[h] + 1 - zfirst[h]])
+        if h != 1:
+            x_wait(pk.at[h], True, ssem.at[flow_down[h] + zfirst[h]], True)
     drain(ws, True, flow_stat, True)
     drain(ws, True, flow_stat + 2, False)
     near_wait(bulk_part, True, ssem.at[near], True)
     near_wait(stat_part, True, ssem.at[near + 2], True)
     near_wait(stat_part, False, ssem.at[near + 3], True)
-    returned(0)
-    returned(1)
+    near_wait(pair_part, False, ssem.at[near_out], True)
     returned(2)
     returned(3)
-    near_wait(bulk_part, False, rsem.at[near + 1], False)
-    finish(0)
-    finish(1)
-    finish(2)
-    finish(3)
+    near_wait(pair_part, False, rsem.at[near_dq], False)
+    finish_queries(0)
+    finish_queries(1)
     for h in range(heads):
         drain(pk.at[h], zfirst[h], flow_up[h], False)
-    near_wait(bulk_part, False, ssem.at[near + 1], True)
+    near_wait(pair_part, False, ssem.at[near_dq], True)
 
 
 def local(mesh_seq, mesh_head, queries, keys, values, dout, selected):
@@ -529,7 +589,7 @@
     lane = np.arange(far)
     spread = jnp.asarray((np.arange(HD)[:, None] == lane[None] % QB).astype(np.float32), BF)
     owner_mask = jnp.asarray((np.arange(zn)[:, None] == lane[None] // QB).astype(np.float32))
-    flows = 4 * heads + 12
+    flows = 4 * heads + 15
     block = lambda groups: pltpu.VMEM((heads, groups, zn, 2 * QB, HD), BF)
     stat = lambda groups: pltpu.VMEM((groups, zn, heads // 2, HD), F32)
     shape = jax.ShapeDtypeStruct((tokens, width), BF)
@@ -541,7 +601,8 @@
         + [pltpu.VMEM((blocks, QB, width), F32)] * 2
         + [pltpu.VMEM((heads, tokens, HD), BF)] * 2
         + [pltpu.VMEM((heads, HD, tokens), BF)] * 2
-        + [block(xn), block(xn), block(xn + 1), block(xn + 1), block(xn), block(xn)]
+        + [block(xn), block(xn), block(xn + 1), block(xn + 1), block(xn)]
+        + [pltpu.VMEM((heads // 2, xn, zn, 2 * QB, HD), BF)] * 2
         + [stat(xn + 1), stat(xn), stat(xn), stat(xn), stat(xn), stat(xn + 1)]
         + [pltpu.VMEM((heads, xn + 1, far, HD), BF)] * 2
         + [pltpu.VMEM((heads, xn + 1, tokens, far), F32)] * 2
@@ -551,8 +612,10 @@
         + [pltpu.VMEM((TOPK + 1, zn, HD), F32)]
         + [pltpu.VMEM((zn, 1, HD), F32)] * 2
         + [pltpu.VMEM((zn, 2 * QB, HD), F32)]
+        + [pltpu.VMEM((heads // 2, xn + 1, zn, QB, HD), F32)]
+        + [pltpu.VMEM((heads // 2, TOPK + 1, HD, zn), F32)]
         + [pltpu.SemaphoreType.DMA((flows,))] * 2
-        + [pltpu.SemaphoreType.DMA((4,))]
+        + [pltpu.SemaphoreType.DMA((6,))]
     )
     return pl.pallas_call(
         functools.partial(kernel, xn, zn, hn, heads),

time: 247 us -> 223 us (0.903)
  the two profiles are of different devices: /device:TPU:456 before, /device:TPU:454 now
where the time goes in v3:
time: 223 us
  Pallas kernels  215 us (96%)
  local copies, waits for them, and re-layouts  6.19 us (3%)
    pallas_call x1, Pallas kernels, local(): pl.pallas_call(functools.partial(kernel, xn, zn, hn, heads), out_shape=(s...  215 us
    unnamed x13, local copies, waits for them, and re-layouts  6.19 us

profile of v3, /device:TPU:454, one launch (start us, length us, event | category | flops | bytes accessed | tf_op | source)
XLA Modules:
  0.0 222.6 jit_solution(8484589970496109201)
XLA Ops:
  0.6 0.0 copy-start.3
  0.6 0.7 copy-done.3
  1.3 0.1 fusion.1
  1.4 0.5 convert_reduce_fusion
  1.9 0.7 copy.14.sel
  2.6 215.1 %shard_map.102 = (bf16[384,512]{1,0:T(8,128)(2,1)}, bf16[384,512]{1,0:T(8,128)(2,1)}, bf16[384,512]{1,0:T(8,128)(2,1)}, bf16[384,512]{1,0:T(8,128)(2,1)}) custom-call(s32[16,3]{1,0:T(8,128)} %copy.14.sel, s32[64]{0:T(128)} %get-tuple-element.5.inv, s32[64]{0:T(128)} %get-tuple-element.4.flag, bf16[128,384]{1,0:T(8,128)(2,1)} %constant.14.clone.spread, ...), custom_call_target="tpu_custom_call" | custom-call | tf_op jit(solution)/shard_map/pallas_call | solution.py:620
  217.8 0.0 copy-start.2
  217.8 1.8 copy.19
  219.6 0.0 copy-done.2
  219.6 0.0 copy-start.1
  219.6 0.7 copy.20
  220.3 0.4 copy-done.1
  220.7 0.0 copy-start
  220.7 0.7 copy.21
  221.5 0.4 copy-done
  221.9 0.7 copy.22
  (1 shorter events, 0.0 us)
Async XLA Ops:
  0.6 0.7 copy-start.3
  217.8 1.8 copy-start.2
  219.6 1.1 copy-start.1
  220.7 1.1 copy-start

commit v4 on v3

--- a/solution.py
+++ b/solution.py
@@ -127,7 +127,7 @@
         if down:
             loop(0, z, body)
         else:
-            loop(z + 1, zn, body)
+            loop(0, zn - 1 - z, lambda i: body(zn - 1 - i))
 
     def near_wait(part, down, sem, sent):
         when(z if down == sent else zn - 1 - z, zn - 1, lambda m: wait(part(m), sem))
@@ -214,10 +214,6 @@
     def drain_heads():
         for n in range(6):
             head_wait(n, ssem.at[flow_head + n])
-
-    f[...] = jnp.zeros_like(f)
-    wr[...] = jnp.zeros_like(wr)
-    sr[...] = jnp.zeros_like(sr)
 
     barrier = pltpu.get_barrier_semaphore()
 
@@ -282,6 +278,14 @@
 
     for n in range(6):
         spread_heads(n)
+
+    def clear(i):
+        wr[x, i] = jnp.zeros((heads // 2, HD), F32)
+        for h in range(heads):
+            f[h, x, i] = jnp.zeros((2 * QB, HD), BF)
+
+    loop(0, z + 1, clear)
+    sr[x, z] = jnp.zeros((heads // 2, HD), F32)
 
     def block_of(i, h):
         cols = slice(h * HD, (h + 1) * HD)
@@ -359,19 +363,21 @@
 
         loop(0, heads // 2, body)
 
-    def statistics(stage, first, last):
-        picks = (2 * stage, 2 * stage + 1, heads + 2 * stage, heads + 2 * stage + 1)
-
+    def picks_of(stage):
+        return (2 * stage, 2 * stage + 1, heads + 2 * stage, heads + 2 * stage + 1)
+
+    def statistics(stages, first, last):
         def to_rows(group):
             mask = owner_mask[...]
-            parts = split3(jnp.concatenate([sv[group, k] * mask for k in picks], axis=0))
-            flat = dot(parts, spread[...], 1, 1)
-            flat = flat[: 4 * zn] + flat[4 * zn : 8 * zn] + flat[8 * zn :]
-            out = flat[:zn]
-            for k in range(1, 4):
-                out = out + pltpu.roll(flat[k * zn : (k + 1) * zn], QB * k, 1)
-            for i in range(zn):
-                su[group, i, pl.ds(stage, 1)] = out[i : i + 1]
+            for stage in stages:
+                lines = [sv[group, k] * mask for k in picks_of(stage)]
+                flat = dot(split3(jnp.concatenate(lines, axis=0)), spread[...], 1, 1)
+                flat = flat[: 4 * zn] + flat[4 * zn : 8 * zn] + flat[8 * zn :]
+                out = flat[:zn]
+                for k in range(1, 4):
+                    out = out + pltpu.roll(flat[k * zn : (k + 1) * zn], QB * k, 1)
+                for i in range(zn):
+                    su[group, i, pl.ds(stage, 1)] = out[i : i + 1]
 
         loop(first, last, to_rows)
 
@@ -412,15 +418,17 @@
 
         loop(0, xn, slots)
 
-    def weights_of(stage):
+    def weights():
         def to_lanes(group):
-            m = jnp.concatenate([wr[group, i, pl.ds(stage, 1)] for i in range(zn)], axis=0)
-            wide = [m] + [pltpu.roll(m, HD - QB * k, 1) for k in range(1, 4)]
-            flat = dot(split3(jnp.concatenate(wide, axis=0)), spread[...], 1, 0)
-            flat = flat[: 4 * zn] + flat[4 * zn : 8 * zn] + flat[8 * zn :]
             mask = owner_mask[...]
-            for k, pick in enumerate((2 * stage, 2 * stage + 1, heads + 2 * stage, heads + 2 * stage + 1)):
-                wv[group, pick] = jnp.sum(flat[k * zn : (k + 1) * zn] * mask, axis=0, keepdims=True)
+            for stage in range(heads // 2):
+                m = jnp.concatenate([wr[group, i, pl.ds(stage, 1)] for i in range(zn)], axis=0)
+                wide = [m] + [pltpu.roll(m, HD - QB * k, 1) for k in range(1, 4)]
+                flat = dot(split3(jnp.concatenate(wide, axis=0)), spread[...], 1, 0)
+                flat = flat[: 4 * zn] + flat[4 * zn : 8 * zn] + flat[8 * zn :]
+                for k, pick in enumerate(picks_of(stage)):
+                    part = flat[k * zn : (k + 1) * zn] * mask
+                    wv[group, pick] = jnp.sum(part, axis=0, keepdims=True)
 
         loop(x, xn + 1, to_lanes)
 
@@ -507,16 +515,15 @@
     scores(0)
     arrived(1)
     scores(1)
-    statistics(0, x + 1, xn + 1)
+    statistics((0,), x + 1, xn + 1)
     pl.when(x == 0)(near_scores)
     arrived(2)
     scores(2)
     arrived(3)
     scores(3)
-    statistics(1, x + 1, xn + 1)
+    statistics((1,), x + 1, xn + 1)
     pl.when(x > 0)(near_scores)
-    statistics(0, x, x + 1)
-    statistics(1, x, x + 1)
+    statistics((0, 1), x, x + 1)
     up_first(su, srx, True, flow_stat + 2)
     near_send(stat_at(su), stat_at(sr), False, near + 3)
     start_up(0)
@@ -533,12 +540,11 @@
     down_second(wrz, wr, True, flow_stat)
     down_done(wrz, wr, True, flow_stat)
     near_wait(stat_part, True, rsem.at[near + 2], False)
-    weights_of(0)
+    weights()
+    gradients(1)
+    start_up(3)
     gradients(0)
     start_up(2)
-    weights_of(1)
-    gradients(1)
-    start_up(3)
     near_send(pair_at(rt, 2), lambda zi: gd.at[:, x, zi], False, near_dq)
     return_relay(1)
     return_relay(2)
@@ -569,6 +575,20 @@
     for h in range(heads):
         drain(pk.at[h], zfirst[h], flow_up[h], False)
     near_wait(pair_part, False, ssem.at[near_dq], True)
+
+
+def settle(a, b, c, d, att, gq, gk, gv, held, sem):
+    inward = [pltpu.make_async_copy(src, held.at[n], sem.at[n]) for n, src in enumerate((a, b, c, d))]
+    outward = [
+        pltpu.make_async_copy(held.at[n], dst, sem.at[4 + n]) for n, dst in enumerate((att, gq, gk, gv))
+    ]
+    for copy in inward:
+        copy.start()
+    for first, second in zip(inward, outward):
+        first.wait()
+        second.start()
+    for copy in outward:
+        copy.wait()
 
 
 def local(mesh_seq, mesh_head, queries, keys, values, dout, selected):
@@ -617,7 +637,7 @@
         + [pltpu.SemaphoreType.DMA((flows,))] * 2
         + [pltpu.SemaphoreType.DMA((6,))]
     )
-    return pl.pallas_call(
+    results = pl.pallas_call(
         functools.partial(kernel, xn, zn, hn, heads),
         out_shape=(shape,) * 4,
         in_specs=[smem] * 3 + [vmem] * 2 + [hbm] * 4,
@@ -627,6 +647,14 @@
             collective_id=0, has_side_effects=True, vmem_limit_bytes=VMEM_LIMIT
         ),
     )(selected, inv, flag, spread, owner_mask, queries, keys, values, dout)
+    return pl.pallas_call(
+        settle,
+        out_shape=(shape,) * 4,
+        in_specs=[hbm] * 4,
+        out_specs=(hbm,) * 4,
+        scratch_shapes=[pltpu.VMEM((4, tokens, width), BF), pltpu.SemaphoreType.DMA((8,))],
+        compiler_params=pltpu.CompilerParams(vmem_limit_bytes=VMEM_LIMIT),
+    )(*results)
 
 
 def solution(mesh):

time: 223 us -> 218 us (0.978)
  local copies, waits for them, and re-layouts: 6.19 us -> 1.35 us
    unnamed x13 -> x3, local copies, waits for them, and re-layouts: 6.19 us -> 1.35 us
    pallas_call x1, Pallas kernels: 215 us -> 213 us  [local(): pl.pallas_call(functools.partial(kernel, xn, zn, hn, heads), out_shape=(s...]
where the time goes in v4:
time: 218 us
  Pallas kernels  215 us (99%)
    pallas_call x1, Pallas kernels, local(): pl.pallas_call(functools.partial(kernel, xn, zn, hn, heads), out_shape=(s...  213 us

profile of v4, /device:TPU:454, one launch (start us, length us, event | category | flops | bytes accessed | tf_op | source)
XLA Modules:
  0.0 217.5 jit_solution(16960989438602446348)
XLA Ops:
  0.6 0.0 copy-start
  0.6 0.7 copy-done
  1.3 0.1 fusion.1
  1.4 0.5 convert_reduce_fusion
  1.9 0.7 copy.14.sel
  2.6 212.7 %shard_map.102 = (bf16[384,512]{1,0:T(8,128)(2,1)}, bf16[384,512]{1,0:T(8,128)(2,1)}, bf16[384,512]{1,0:T(8,128)(2,1)}, bf16[384,512]{1,0:T(8,128)(2,1)}) custom-call(s32[16,3]{1,0:T(8,128)} %copy.14.sel, s32[64]{0:T(128)} %get-tuple-element.13.inv, s32[64]{0:T(128)} %get-tuple-element.12.flag, bf16[128,384]{1,0:T(8,128)(2,1)} %constant.14.clone.spread, ...), custom_call_target="tpu_custom_call" | custom-call | tf_op jit(solution)/shard_map/pallas_call | solution.py:640
  215.3 2.2 %shard_map.103 = (bf16[384,512]{1,0:T(8,128)(2,1)}, bf16[384,512]{1,0:T(8,128)(2,1)}, bf16[384,512]{1,0:T(8,128)(2,1)}, bf16[384,512]{1,0:T(8,128)(2,1)}) custom-call(bf16[384,512]{1,0:T(8,128)(2,1)} %get-tuple-element.8.a, bf16[384,512]{1,0:T(8,128)(2,1)} %get-tuple-element.9.b, bf16[384,512]{1,0:T(8,128)(2,1)} %get-tuple-element.10.c, ...), custom_call_target="tpu_custom_call" | custom-call | tf_op jit(solution)/shard_map/pallas_call | solution.py:650
  (1 shorter events, 0.0 us)
Async XLA Ops:
  0.6 0.7 copy-start
